TPU v7x, 512 devices: a whole 4x4x16 slice. The times are simulated.
512 devices in a mesh: ex: 16 (over y, z_hi), par: 32 (over x, z_lo, core).
Axes of the slice: x: 4, y: 4, z: 16 (z_hi: 4, z_lo: 4; z = z_hi * 4 + z_lo), core: 2. Of those that a mesh axis runs over, the one named last changes fastest.
Arguments:
- normed_hidden_input: bfloat16 [64, 128, 4096], P('ex', None, 'par'), may hold values from -6 to 6
- attention_output: bfloat16 [64, 128, 4096], P('ex', None, 'par'), may hold values from -6 to 6
- query_output_gradient: bfloat16 [64, 128, 4096], P('ex', None, 'par'), may hold values from -6 to 6
- key_output_gradient: bfloat16 [64, 128, 4096], P('ex', None, 'par'), may hold values from -6 to 6
- value_output_gradient: bfloat16 [64, 128, 4096], P('ex', None, 'par'), may hold values from -6 to 6
- out_projection_gradient: bfloat16 [64, 128, 4096], P('ex', None, 'par'), may hold values from -6 to 6
- adapter_down_weight: bfloat16 [4, 128, 4096], P(None, 'ex', 'par'), may hold values from -0.09375 to 0.09375
- adapter_up_weight: bfloat16 [4, 4096, 128], P(None, 'par', 'ex'), may hold values from -0.09375 to 0.09375
- up_left_factor: bfloat16 [4, 4096, 64], P(None, 'par'), may hold values from -0.09375 to 0.09375
- up_right_factor: bfloat16 [4, 128, 128], replicated, may hold values from -0.5 to 0.5
- down_left_factor: bfloat16 [4, 128, 64], replicated, may hold values from -0.5 to 0.5
- down_right_factor: bfloat16 [4, 4096, 128], P(None, 'par'), may hold values from -0.09375 to 0.09375
Outputs:
- features: float32 [64, 8192], P('ex', 'par')
All inputs are finite; a program needn't handle non-finite values.
Results may differ from a plain program's by a relative error of at most 0.005.
Values may be sent and summed in bfloat16 or wider, within the bound.
No kernel may reach another device: no remote copies, remote signals or barrier semaphores. Data moves between devices by JAX's collectives and lax.ppermute only.
A program may use at most 64 MiB of HBM per device.

v0:
```python
import jax
import jax.numpy as jnp
from jax import lax
from jax.sharding import PartitionSpec as P


def project(tok_rows, weight):
    return jnp.dot(tok_rows, weight, preferred_element_type=jnp.float32)


def per_device(
    normed_hidden_input,
    attention_output,
    query_output_gradient,
    key_output_gradient,
    value_output_gradient,
    out_projection_gradient,
    adapter_down_weight,
    adapter_up_weight,
    up_left_factor,
    up_right_factor,
    down_left_factor,
    down_right_factor,
):
    groups, length, feat_width = normed_hidden_input.shape
    tok_count = groups * length
    cols_x = up_right_factor.shape[2]
    cols_g = up_left_factor.shape[2]
    down_full, up_full = (
        lax.all_gather(adapter_down_weight, "ex", axis=1, tiled=True),
        lax.all_gather(adapter_up_weight, "ex", axis=2, tiled=True),
    )
    input_side = jnp.einsum(
        "oyt,oyj->otj", down_full, up_right_factor, preferred_element_type=jnp.float32
    )
    gradient_side = jnp.einsum(
        "ibc,icl->ibl", up_full, down_left_factor, preferred_element_type=jnp.float32
    )
    w_x = jnp.concatenate([input_side.astype(jnp.bfloat16), down_right_factor], axis=2)
    w_g = jnp.concatenate([up_left_factor, gradient_side.astype(jnp.bfloat16)], axis=2)
    hidden_rows = normed_hidden_input.reshape(tok_count, feat_width)
    attn_rows = attention_output.reshape(tok_count, feat_width)
    grad_rows = (
        query_output_gradient.reshape(tok_count, feat_width),
        key_output_gradient.reshape(tok_count, feat_width),
        value_output_gradient.reshape(tok_count, feat_width),
        out_projection_gradient.reshape(tok_count, feat_width),
    )
    x_total = 2 * cols_x
    shared = project(hidden_rows, jnp.concatenate([w_x[0], w_x[1], w_x[2]], axis=1))
    pieces = [shared, project(attn_rows, w_x[3])] + [
        project(grad_rows[module_id], w_g[module_id]) for module_id in range(4)
    ]
    summed = lax.psum_scatter(
        jnp.concatenate(pieces, axis=1), "par", scatter_dimension=0, tiled=True
    )
    x_sum = summed[:, : 4 * x_total]
    g_sum = summed[:, 4 * x_total :]
    rows_here = x_sum.shape[0]
    x_vals = x_sum.astype(jnp.bfloat16).reshape(rows_here, 8, cols_x)
    g_vals = g_sum.astype(jnp.bfloat16).reshape(rows_here, 8, cols_g)
    position = lax.axis_index("par") * rows_here + jnp.arange(rows_here, dtype=jnp.int32)
    owner = position // length
    onehot = (owner[:, None] == jnp.arange(groups, dtype=jnp.int32)[None, :]).astype(jnp.bfloat16)
    weighted = g_vals[:, None, :, :] * onehot[:, :, None, None]
    feature = jnp.einsum(
        "tebi,tbj->eij", weighted, x_vals, preferred_element_type=jnp.float32
    ).reshape(groups, cols_g * cols_x)
    reduced = lax.psum_scatter(feature, "par", scatter_dimension=1, tiled=True)
    return reduced * (1.0 / length)


def solution(mesh):
    in_specs = (
        P("ex", None, "par"),
        P("ex", None, "par"),
        P("ex", None, "par"),
        P("ex", None, "par"),
        P("ex", None, "par"),
        P("ex", None, "par"),
        P(None, "ex", "par"),
        P(None, "par", "ex"),
        P(None, "par", None),
        P(),
        P(),
        P(None, "par", None),
    )
    out_specs = P("ex", "par")
    return jax.shard_map(
        per_device, mesh=mesh, in_specs=in_specs, out_specs=out_specs, check_vma=False
    )
```

profile of v0, /device:TPU:1, one launch (start us, length us, event | category | flops | bytes accessed | tf_op | source)
XLA Modules:
  0.0 433.5 jit_solution(4025237654496587815)
XLA Ops:
  6.5 0.0 copy-start
  6.5 0.0 copy-start.6
  6.5 0.0 copy-start.1
  6.5 0.0 reduce-scatter.7.cloned.1.call-start
  6.5 53.2 %all_gather.6 = bf16[4,128,128]{2,1,0:T(8,128)(2,1)S(1)} all-gather(bf16[4,8,128]{2,1,0:T(8,128)(2,1)} %param.18), channel_id=1, replica_groups=mesh['ex'=16,'par'=32] {'ex'}, dimensions={1}, use_global_device_ids=true | all-gather | bytes 139264 | tf_op jit(solution)/shard_map/all_gather | solution.py:30
  59.7 1.0 copy.21
  60.8 0.0 copy-start.2
  60.8 0.0 copy-start.3
  60.8 0.0 copy-start.4
  60.8 0.0 copy-start.5
  60.8 40.8 %all_gather.7 = bf16[4,128,128]{1,2,0:T(8,128)(2,1)S(1)} all-gather(bf16[4,128,8]{1,2,0:T(8,128)(2,1)} %param.19), channel_id=1, replica_groups=mesh['ex'=16,'par'=32] {'ex'}, dimensions={2}, use_global_device_ids=true | all-gather | bytes 139264 | tf_op jit(solution)/shard_map/all_gather | solution.py:31
  101.6 1.1 convolution_convert_fusion
  102.8 0.0 copy-done
  102.8 0.4 bitcast_dynamic-update-slice_fusion
  103.1 1.1 fusion
  104.3 0.0 copy-done.6
  104.3 0.1 convolution_convert_fusion.1
  104.4 0.0 copy-done.1
  104.5 0.0 copy-done.2
  104.5 0.2 fusion.4
  104.7 0.0 copy-done.3
  104.7 0.2 fusion.3
  104.9 0.0 copy-done.4
  104.9 0.2 fusion.2
  105.1 0.0 copy-done.5
  105.1 0.2 fusion.1
  105.3 2.3 copy.29
  107.6 0.0 reduce-scatter.7.cloned.1.call-update
  107.6 0.0 reduce-scatter.9.cloned.1.call-start
  107.7 158.5 %reduce-scatter.7.cloned.1.call-done = f32[16,1536]{1,0:T(8,128)} async-done(((f32[512,1536]{1,0:T(8,128)}), f32[16,1536]{1,0:T(8,128)}) %reduce-scatter.7.cloned.1.call-update) | async-done | bytes 98320
  266.2 0.8 slice.55
  267.0 0.2 copy.34
  267.2 0.8 slice.54
  268.0 0.1 copy.35
  268.1 0.1 copy.22
  268.2 0.5 convolution_bitcast_fusion.5
  268.7 2.6 copy.33
  271.3 0.0 reduce-scatter.9.cloned.1.call-update
  271.4 153.7 %reduce-scatter.9.cloned.1.call-done = f32[256,4]{1,0:T(8,128)} async-done(((f32[8192,4]{1,0:T(8,128)}), f32[256,4]{1,0:T(8,128)}) %reduce-scatter.9.cloned.1.call-update) | async-done | bytes 4112
  425.0 1.0 copy.32
  426.0 0.6 broadcast_multiply_fusion
  (3 shorter events, 0.0 us)
Async XLA Ops:
  6.5 96.2 %copy-start = (bf16[4,128,128]{2,1,0:T(8,128)(2,1)S(1)}, bf16[4,128,128]{2,1,0:T(8,128)(2,1)}, u32[]{:S(2)}) copy-start(bf16[4,128,128]{2,1,0:T(8,128)(2,1)} %param.12) | copy-start | bytes 393220
  6.5 97.7 %copy-start.6 = (bf16[4,128,64]{1,2,0:T(8,128)(2,1)S(1)}, bf16[4,128,64]{1,2,0:T(8,128)(2,1)}, u32[]{:S(2)}) copy-start(bf16[4,128,64]{1,2,0:T(8,128)(2,1)} %param.22) | copy-start | bytes 196612
  6.5 97.9 %copy-start.1 = (bf16[4,128,64]{1,2,0:T(8,128)(2,1)S(1)}, bf16[4,128,64]{1,2,0:T(8,128)(2,1)}, u32[]{:S(2)}) copy-start(bf16[4,128,64]{1,2,0:T(8,128)(2,1)} %param.20) | copy-start | bytes 196612
  6.5 259.7 %reduce-scatter.7.cloned.1.call-start = ((), (), s32[]{:S(2)}) async-start(), calls=%async_computation.2 | async-start | bytes 3244032
  60.8 43.7 %copy-start.2 = (bf16[4,128,128]{2,1,0:T(8,128)(2,1)S(1)}, bf16[4,128,128]{2,1,0:T(8,128)(2,1)}, u32[]{:S(2)}) copy-start(bf16[4,128,128]{2,1,0:T(8,128)(2,1)} %param.14) | copy-start | bytes 393220
  60.8 43.9 %copy-start.3 = (bf16[4,128,128]{2,1,0:T(8,128)(2,1)S(1)}, bf16[4,128,128]{2,1,0:T(8,128)(2,1)}, u32[]{:S(2)}) copy-start(bf16[4,128,128]{2,1,0:T(8,128)(2,1)} %param.15) | copy-start | bytes 393220
  60.8 44.1 %copy-start.4 = (bf16[4,128,128]{2,1,0:T(8,128)(2,1)S(1)}, bf16[4,128,128]{2,1,0:T(8,128)(2,1)}, u32[]{:S(2)}) copy-start(bf16[4,128,128]{2,1,0:T(8,128)(2,1)} %param.16) | copy-start | bytes 393220
  60.8 44.3 %copy-start.5 = (bf16[4,128,128]{2,1,0:T(8,128)(2,1)S(1)}, bf16[4,128,128]{2,1,0:T(8,128)(2,1)}, u32[]{:S(2)}) copy-start(bf16[4,128,128]{2,1,0:T(8,128)(2,1)} %param.17) | copy-start | bytes 393220
  107.6 317.4 %reduce-scatter.9.cloned.1.call-start = ((), (), s32[]{:S(2)}) async-start(), calls=%async_computation.3 | async-start | bytes 4325376
Sparse Core Ops, SparseCore 0:
  107.8 158.3 reduce-scatter.6
  271.5 153.5 reduce-scatter.8
where the time goes:
time: 437 us; the launch traced here: 433 us
  waiting for transfers between devices  312 us (71%)
  blocking collectives  94 us (22%)
  between operations  13.6 us (3%)
  local copies, waits for them, and re-layouts  9.03 us (2%)
    unnamed x4, waiting for transfers between devices  312 us
    all_gather x1, blocking collectives, per_device(): lax.all_gather(adapter_down_weight, 'ex', axis=1, tiled=True)  53.2 us
    all_gather x1, blocking collectives, per_device(): lax.all_gather(adapter_up_weight, 'ex', axis=2, tiled=True)  40.8 us
  transfers between devices with their start and end apart: 2, of which 2 were waited for; matrix products, arithmetic and copies ran while one was open for 0% of the time, Pallas kernels for 0%

commit v1 on v0

v1 whole, which is shorter than its diff:
```python
import jax
import jax.numpy as jnp
from jax import lax
from jax.sharding import PartitionSpec as P

BF = jnp.bfloat16
F32 = jnp.float32

CHIPS = [[2 * chip + core for chip in range(16)] for core in range(2)]
Z_HI = [[4 * y + z for z in range(4)] for y in range(4)]
Y = [[4 * y + z for y in range(4)] for z in range(4)]
PAIR = [(i, i ^ 1) for i in range(32)]


def mm(a, b):
    return jnp.dot(a, b, preferred_element_type=F32)


def spread(block, axis, groups):
    count = len(groups[0])
    copies = jnp.broadcast_to(block[None], (count,) + block.shape)
    return lax.all_to_all(copies, axis, 0, 0, tiled=True, axis_index_groups=groups)


def per_device(
    hidden,
    attn,
    grad_q,
    grad_k,
    grad_v,
    grad_o,
    adapter_down,
    adapter_up,
    up_left,
    up_right,
    down_left,
    down_right,
):
    core = lax.axis_index("par") % 2

    shard = jnp.concatenate(
        [adapter_down.reshape(32, 128), adapter_up.transpose(0, 2, 1).reshape(32, 128)]
    )
    along_z = spread(shard, "ex", Z_HI).reshape(256, 128)
    gathered = spread(along_z, "ex", Y).reshape(16, 2, 4, 8, 128)
    gathered = gathered.transpose(1, 2, 0, 3, 4).reshape(2, 4, 128, 128)
    side_x = jnp.einsum("orf,orj->ofj", gathered[0], up_right, preferred_element_type=F32)
    side_g = jnp.einsum("irf,irl->ifl", gathered[1], down_left, preferred_element_type=F32)
    side_x = side_x.astype(BF)
    side_g = side_g.astype(BF)
    side = jnp.concatenate(
        [
            side_x,
            jnp.concatenate([side_g[0], side_g[1]], axis=1)[None],
            jnp.concatenate([side_g[2], side_g[3]], axis=1)[None],
        ]
    )
    side_other = lax.ppermute(side, "par", PAIR)

    inputs = [hidden, attn, grad_q, grad_k, grad_v, grad_o]
    keep = [lax.dynamic_slice_in_dim(a, 2 * core, 2, 0) for a in inputs]
    send = [lax.dynamic_slice_in_dim(a, 2 - 2 * core, 2, 0) for a in inputs]
    ul = [
        jnp.concatenate([up_left[0], up_left[1]], axis=1)[None],
        jnp.concatenate([up_left[2], up_left[3]], axis=1)[None],
    ]
    other = lax.ppermute(jnp.concatenate(send + ul + [down_right]), "par", PAIR)
    rows = [
        jnp.concatenate([keep[k], other[2 * k : 2 * k + 2]], axis=2).reshape(256, 256)
        for k in range(6)
    ]
    h_rows, a_rows, g_rows = rows[0], rows[1], rows[2:]
    dr = jnp.concatenate([down_right, other[14:18]], axis=1)
    ul_all = jnp.concatenate([jnp.concatenate(ul), other[12:14]], axis=1)
    ul_of = [ul_all[m // 2][:, 64 * (m % 2) : 64 * (m % 2) + 64] for m in range(4)]

    x_right = [mm(h_rows, jnp.concatenate([dr[0], dr[1], dr[2]], axis=1)), mm(a_rows, dr[3])]
    g_left = [mm(g_rows[m], ul_of[m]) for m in range(4)]
    part = jnp.concatenate([p.astype(BF) for p in x_right + g_left], axis=1)
    pieces = lax.all_to_all(
        part.reshape(16, 16, 768), "par", 0, 0, tiled=True, axis_index_groups=CHIPS
    )
    total = jnp.sum(pieces.astype(F32), axis=0).astype(BF)
    full = spread(total, "par", CHIPS).reshape(2, 128, 768)

    sx = jnp.concatenate([side_x, side_other[:4]], axis=1)
    sg_all = jnp.concatenate([side[4:], side_other[4:]], axis=1)
    sg = [sg_all[m // 2][:, 64 * (m % 2) : 64 * (m % 2) + 64] for m in range(4)]
    x_left = jnp.concatenate(
        [mm(h_rows, jnp.concatenate([sx[0], sx[1], sx[2]], axis=1)), mm(a_rows, sx[3])], axis=1
    ).astype(BF)
    g_right = [mm(g_rows[m], sg[m]).astype(BF) for m in range(4)]
    x_all = jnp.concatenate(
        [x_left.reshape(2, 128, 4, 128), full[:, :, :512].reshape(2, 128, 4, 128)], axis=2
    )
    g_all = jnp.concatenate(
        [
            full[:, :, 512:].reshape(2, 128, 4, 64),
            jnp.stack(g_right, axis=1).reshape(2, 128, 4, 64),
        ],
        axis=2,
    )
    raw = jnp.einsum("etbi,etbj->eij", g_all, x_all, preferred_element_type=F32)
    out = raw.reshape(2, 32, 256).transpose(1, 0, 2)
    out = lax.all_to_all(out, "par", 0, 0, tiled=True)
    out = jnp.sum(out.reshape(16, 4, 256), axis=0)
    return out * (1.0 / 128)


def solution(mesh):
    in_specs = (P("ex", None, "par"),) * 6 + (
        P(None, "ex", "par"),
        P(None, "par", "ex"),
        P(None, "par", None),
        P(),
        P(),
        P(None, "par", None),
    )
    return jax.shard_map(
        per_device, mesh=mesh, in_specs=in_specs, out_specs=P("ex", "par"), check_vma=False
    )
```

time: 437 us -> 97.1 us (0.22)
  waiting for transfers between devices: 312 us -> 15.4 us
  blocking collectives: 94 us -> 34.9 us
  starting transfers between devices: 0.04 us -> 29.8 us
  between operations: 13.6 us -> 0.49 us
    unnamed x4 -> x0, waiting for transfers between devices: 312 us -> none
    all_gather x2 -> x0, blocking collectives: 94 us -> none  [the longest x1 53.2 us: per_device(): lax.all_gather(adapter_down_weight, 'ex', axis=1, tiled=True)]
    all_to_all x0 -> x2, blocking collectives: none -> 34.9 us  [the longest x1 21.1 us: spread(): lax.all_to_all(copies, axis, 0, 0, tiled=True, axis_index_groups=groups)]
    all_to_all x0 -> x3, starting transfers between devices: none -> 15.3 us  [the longest x2 9.81 us: spread(): lax.all_to_all(copies, axis, 0, 0, tiled=True, axis_index_groups=groups)]
    ppermute x0 -> x2, starting transfers between devices: none -> 14.5 us  [the longest x1 8.79 us: per_device(): other = lax.ppermute(jnp.concatenate(send + ul + [down_right]), 'par', PAIR)]
    all_to_all x0 -> x3, waiting for transfers between devices: none -> 14.4 us  [the longest x2 12.7 us: spread(): lax.all_to_all(copies, axis, 0, 0, tiled=True, axis_index_groups=groups)]
  transfers between devices with their start and end apart: 2 -> 5, of which waited for: 2 -> 4; matrix products, arithmetic and copies ran while one was open for 0% -> 6% of each run, Pallas kernels for 0% -> 0%
where the time goes in v1:
time: 97.1 us; the launch traced here: 96.3 us
  blocking collectives  34.9 us (36%)
  starting transfers between devices  29.8 us (31%)
  waiting for transfers between devices  15.4 us (16%)
  local copies, waits for them, and re-layouts  11.7 us (12%)
  matrix products  2.97 us (3%)
  other arithmetic  1.13 us (1%)
    all_to_all x1, blocking collectives, spread(): lax.all_to_all(copies, axis, 0, 0, tiled=True, axis_index_groups=groups)  21.1 us
    all_to_all x1, blocking collectives, per_device(): out = lax.all_to_all(out, 'par', 0, 0, tiled=True)  13.8 us
    all_to_all x2, waiting for transfers between devices, spread(): lax.all_to_all(copies, axis, 0, 0, tiled=True, axis_index_groups=groups)  12.7 us
    all_to_all x2, starting transfers between devices, spread(): lax.all_to_all(copies, axis, 0, 0, tiled=True, axis_index_groups=groups)  9.81 us
    ppermute x1, starting transfers between devices, per_device(): other = lax.ppermute(jnp.concatenate(send + ul + [down_right]), 'par', PAIR)  8.79 us
    unnamed x30, local copies, waits for them, and re-layouts  6.89 us
    ppermute x1, starting transfers between devices, per_device(): side_other = lax.ppermute(side, 'par', PAIR)  5.7 us
    all_to_all x1, starting transfers between devices, per_device(): lax.all_to_all(part.reshape(16, 16, 768), 'par', 0, 0, tiled=True, axis_i...  5.48 us
  transfers between devices with their start and end apart: 5, of which 4 were waited for; matrix products, arithmetic and copies ran while one was open for 6% of the time, Pallas kernels for 0%

profile of v1, /device:TPU:1, one launch (start us, length us, event | category | flops | bytes accessed | tf_op | source)
XLA Modules:
  0.0 96.3 jit_solution(8896768729204908741)
XLA Ops:
  0.0 0.0 copy-start
  0.0 0.8 fusion.50
  0.8 0.0 copy-start.2
  0.8 0.1 copy.82
  0.9 0.1 copy.81
  1.1 0.1 copy.84
  1.2 0.1 copy.83
  1.3 0.4 copy-done.2
  1.7 0.9 copy-done.3
  2.6 0.9 copy-done.4
  3.5 0.9 copy-done.5
  4.4 0.9 copy-done.6
  5.4 0.9 copy-done.7
  6.3 0.0 copy-start.1
  6.3 0.1 constant_dynamic-update-slice_fusion.2
  6.4 0.1 constant_dynamic-update-slice_fusion.1
  6.5 0.7 copy-done.1
  7.2 8.8 %collective-permute-start = (bf16[18,128,128]{2,1,0:T(8,128)(2,1)S(1)}, bf16[18,128,128]{2,1,0:T(8,128)(2,1)S(1)}, u32[]{:S(2)}, u32[]{:S(2)}) collective-permute-start(bf16[18,128,128]{2,1,0:T(8,128)(2,1)S(1)} %constant_dynamic-update-slice_fusion), channel_id=1, source_target_pairs={{0,1},{1,0},{2,3},{3,2},{4,5},{5,4},{6,7},{7,6},{8,9},{9,8},{10,11... | collective-permute-start | bytes 1769480 | tf_op jit(solution)/shard_map/ppermute | solution.py:67
  16.0 0.0 copy-done.9
  16.0 0.0 copy-done.10
  16.0 21.1 %all_to_all.25 = bf16[4,64,128]{2,1,0:T(8,128)(2,1)S(1)} all-to-all(bf16[4,64,128]{2,1,0:T(8,128)(2,1)S(1)} %broadcast_in_dim.34), channel_id=1, replica_groups={{0,32,64,96},{128,160,192,224},{256,288,320,352},{384,416,448,480},{1,3..., dimensions={0} | all-to-all | bytes 131072 | tf_op jit(solution)/shard_map/all_to_all | solution.py:22
  37.1 0.7 broadcast_in_dim.36
  37.8 4.2 %all-to-all-start.3 = ((bf16[4,256,128]{2,1,0:T(8,128)(2,1)}), bf16[4,256,128]{2,1,0:T(8,128)(2,1)S(1)}, u32[]{:S(2)}, u32[]{:S(2)}) async-start(bf16[4,256,128]{2,1,0:T(8,128)(2,1)} %broadcast_in_dim.36), calls=%async_computation.3 | async-start | bytes 524288 | tf_op jit(solution)/shard_map/all_to_all | solution.py:22
  42.0 0.0 collective-permute-done
  42.2 0.2 convolution_convert_fusion.13
  42.4 0.1 copy.58
  42.5 0.3 convolution_convert_fusion.12
  42.8 0.1 copy.59
  42.9 0.2 convolution_convert_fusion.11
  43.1 0.1 copy.60
  43.3 0.3 convolution_convert_fusion.10
  43.5 0.1 copy.61
  43.7 0.2 convolution_convert_fusion.1
  43.9 0.2 convolution_convert_fusion.5
  44.1 0.9 concatenate.91
  45.0 2.5 %all-to-all-done.3 = bf16[4,256,128]{2,1,0:T(8,128)(2,1)S(1)} async-done(((bf16[4,256,128]{2,1,0:T(8,128)(2,1)}), bf16[4,256,128]{2,1,0:T(8,128)(2,1)S(1)}, u32[]{:S(2)}, u32[]{:S(2)}) %all-to-all-start.3) | async-done | bytes 262176 | tf_op jit(solution)/shard_map/all_to_all | solution.py:22
  47.5 5.5 %all-to-all-start = ((bf16[16,16,768]{2,1,0:T(8,128)(2,1)}), bf16[16,16,768]{2,1,0:T(8,128)(2,1)S(1)}, u32[]{:S(2)}, u32[]{:S(2)}) async-start(bf16[16,16,768]{2,1,0:T(8,128)(2,1)} %bitcast.18), calls=%async_computation | async-start | bytes 786432 | tf_op jit(solution)/shard_map/all_to_all | solution.py:80
  53.0 0.0 copy-start.8
  53.1 0.8 copy-done.8
  53.9 0.1 convolution_convert_fusion.3
  54.1 0.0 copy-done
  54.1 0.2 convolution_convert_fusion.2
  54.4 5.7 %collective-permute-start.1 = (bf16[6,128,128]{1,2,0:T(8,128)(2,1)S(1)}, bf16[6,128,128]{1,2,0:T(8,128)(2,1)S(1)}, u32[]{:S(2)}, u32[]{:S(2)}) collective-permute-start(bf16[6,128,128]{1,2,0:T(8,128)(2,1)S(1)} %pad_maximum_fusion.1), channel_id=1, source_target_pairs={{0,1},{1,0},{2,3},{3,2},{4,5},{5,4},{6,7},{7,6},{8,9},{9,8},{10,11... | collective-permute-start | bytes 589832 | tf_op jit(solution)/shard_map/ppermute | solution.py:58
  60.1 1.0 %collective-permute-done.1 = bf16[6,128,128]{1,2,0:T(8,128)(2,1)S(1)} collective-permute-done((bf16[6,128,128]{1,2,0:T(8,128)(2,1)S(1)}, bf16[6,128,128]{1,2,0:T(8,128)(2,1)S(1)}, u32[]{:S(2)}, u32[]{:S(2)}) %collective-permute-start.1) | collective-permute-done | bytes 196640 | tf_op jit(solution)/shard_map/ppermute | solution.py:58
  61.2 1.6 %all-to-all-done = bf16[16,16,768]{2,1,0:T(8,128)(2,1)S(1)} async-done(((bf16[16,16,768]{2,1,0:T(8,128)(2,1)}), bf16[16,16,768]{2,1,0:T(8,128)(2,1)S(1)}, u32[]{:S(2)}, u32[]{:S(2)}) %all-to-all-start) | async-done | bytes 393248 | tf_op jit(solution)/shard_map/all_to_all | solution.py:80
  62.8 0.1 reduce_sum.21
  62.9 0.8 broadcast_in_dim.33
  63.6 5.6 %all-to-all-start.1 = ((bf16[16,16,768]{2,1,0:T(8,128)(2,1)}), bf16[16,16,768]{2,1,0:T(8,128)(2,1)S(1)}, u32[]{:S(2)}, u32[]{:S(2)}) async-start(bf16[16,16,768]{2,1,0:T(8,128)(2,1)} %broadcast_in_dim.33), calls=%async_computation.1 | async-start | bytes 786432 | tf_op jit(solution)/shard_map/all_to_all | solution.py:22
  69.3 0.2 convolution_convert_fusion.9
  69.5 0.2 convolution_convert_fusion.8
  69.7 0.2 convolution_convert_fusion.7
  69.9 0.2 convolution_convert_fusion.6
  70.1 0.2 convolution_convert_fusion.4
  70.3 0.3 convolution_convert_fusion
  70.6 0.1 convert_element_type.55
  70.7 10.2 %all-to-all-done.1 = bf16[16,16,768]{2,1,0:T(8,128)(2,1)S(1)} async-done(((bf16[16,16,768]{2,1,0:T(8,128)(2,1)}), bf16[16,16,768]{2,1,0:T(8,128)(2,1)S(1)}, u32[]{:S(2)}, u32[]{:S(2)}) %all-to-all-start.1) | async-done | bytes 393248 | tf_op jit(solution)/shard_map/all_to_all | solution.py:22
  81.0 0.1 copy.62
  81.1 0.2 copy.72
  81.3 0.2 copy.74
  81.6 0.2 convolution_bitcast_fusion
  81.8 0.1 copy.98
  81.9 13.8 %all_to_all.26 = f32[32,2,256]{2,1,0:T(2,128)S(1)} all-to-all(f32[32,2,256]{2,1,0:T(2,128)S(1)} %bitcast.117), channel_id=1, replica_groups=mesh['ex'=16,'par'=32] {'par'}, dimensions={0} | all-to-all | bytes 131072 | tf_op jit(solution)/shard_map/all_to_all | solution.py:105
  95.7 0.1 reshape.79
  95.7 0.6 broadcast_multiply_fusion
  (48 shorter events, 0.9 us)
Async XLA Ops:
  0.0 54.1 %copy-start = (bf16[4,128,128]{2,1,0:T(8,128)(2,1)S(1)}, bf16[4,128,128]{2,1,0:T(8,128)(2,1)}, u32[]{:S(2)}) copy-start(bf16[4,128,128]{2,1,0:T(8,128)(2,1)} %param.21) | copy-start | bytes 393220
  0.8 0.9 copy-start.2
  1.7 0.9 copy-start.3
  2.6 0.9 copy-start.4
  3.5 0.9 copy-start.5
  4.4 0.9 copy-start.6
  5.3 0.9 copy-start.7
  6.3 0.9 copy-start.1
  7.2 8.8 %copy-start.9 = (bf16[4,128,8]{1,2,0:T(8,128)(2,1)S(1)}, bf16[4,128,8]{1,2,0:T(8,128)(2,1)}, u32[]{:S(2)}) copy-start(bf16[4,128,8]{1,2,0:T(8,128)(2,1)} %param.19) | copy-start | bytes 24580
  7.2 8.8 %copy-start.10 = (bf16[4,8,128]{2,1,0:T(8,128)(2,1)S(1)}, bf16[4,8,128]{2,1,0:T(8,128)(2,1)}, u32[]{:S(2)}) copy-start(bf16[4,8,128]{2,1,0:T(8,128)(2,1)} %param.18) | copy-start | bytes 24580
  7.2 34.8 %collective-permute-start = (bf16[18,128,128]{2,1,0:T(8,128)(2,1)S(1)}, bf16[18,128,128]{2,1,0:T(8,128)(2,1)S(1)}, u32[]{:S(2)}, u32[]{:S(2)}) collective-permute-start(bf16[18,128,128]{2,1,0:T(8,128)(2,1)S(1)} %constant_dynamic-update-slice_fusion), channel_id=1, source_target_pairs={{0,1},{1,0},{2,3},{3,2},{4,5},{5,4},{6,7},{7,6},{8,9},{9,8},{10,11... | collective-permute-start | bytes 1769480 | tf_op jit(solution)/shard_map/ppermute | solution.py:67
  37.8 9.7 %all-to-all-start.3 = ((bf16[4,256,128]{2,1,0:T(8,128)(2,1)}), bf16[4,256,128]{2,1,0:T(8,128)(2,1)S(1)}, u32[]{:S(2)}, u32[]{:S(2)}) async-start(bf16[4,256,128]{2,1,0:T(8,128)(2,1)} %broadcast_in_dim.36), calls=%async_computation.3 | async-start | bytes 524288 | tf_op jit(solution)/shard_map/all_to_all | solution.py:22
  47.5 15.2 %all-to-all-start = ((bf16[16,16,768]{2,1,0:T(8,128)(2,1)}), bf16[16,16,768]{2,1,0:T(8,128)(2,1)S(1)}, u32[]{:S(2)}, u32[]{:S(2)}) async-start(bf16[16,16,768]{2,1,0:T(8,128)(2,1)} %bitcast.18), calls=%async_computation | async-start | bytes 786432 | tf_op jit(solution)/shard_map/all_to_all | solution.py:80
  53.0 0.8 copy-start.8
  54.4 6.8 %collective-permute-start.1 = (bf16[6,128,128]{1,2,0:T(8,128)(2,1)S(1)}, bf16[6,128,128]{1,2,0:T(8,128)(2,1)S(1)}, u32[]{:S(2)}, u32[]{:S(2)}) collective-permute-start(bf16[6,128,128]{1,2,0:T(8,128)(2,1)S(1)} %pad_maximum_fusion.1), channel_id=1, source_target_pairs={{0,1},{1,0},{2,3},{3,2},{4,5},{5,4},{6,7},{7,6},{8,9},{9,8},{10,11... | collective-permute-start | bytes 589832 | tf_op jit(solution)/shard_map/ppermute | solution.py:58
  63.6 17.3 %all-to-all-start.1 = ((bf16[16,16,768]{2,1,0:T(8,128)(2,1)}), bf16[16,16,768]{2,1,0:T(8,128)(2,1)S(1)}, u32[]{:S(2)}, u32[]{:S(2)}) async-start(bf16[16,16,768]{2,1,0:T(8,128)(2,1)} %broadcast_in_dim.33), calls=%async_computation.1 | async-start | bytes 786432 | tf_op jit(solution)/shard_map/all_to_all | solution.py:22

commit v2 on v1

v2 whole, which is shorter than its diff:
```python
import jax
import jax.numpy as jnp
from jax import lax
from jax.experimental import pallas as pl
from jax.experimental.pallas import tpu as pltpu
from jax.sharding import PartitionSpec as P

BF = jnp.bfloat16
F32 = jnp.float32

CHIPS = [[2 * chip + core for chip in range(16)] for core in range(2)]
Z_HI = [[4 * y + z for z in range(4)] for y in range(4)]
Y = [[4 * y + z for y in range(4)] for z in range(4)]
PAIR = [(i, i ^ 1) for i in range(32)]
VMEM = pl.BlockSpec(memory_space=pltpu.VMEM)
HBM = pl.BlockSpec(memory_space=pl.ANY)


def call(kernel, outs, *operands, specs=None, scratch=()):
    specs = specs or [VMEM] * len(operands)
    operands = [
        pltpu.with_memory_space_constraint(a, pltpu.VMEM) if spec is VMEM else a
        for a, spec in zip(operands, specs)
    ]
    return pl.pallas_call(
        kernel,
        out_shape=tuple(pltpu.VMEM(shape, dtype) for shape, dtype in outs),
        in_specs=specs,
        out_specs=(VMEM,) * len(outs),
        scratch_shapes=scratch,
        name=kernel.__name__,
    )(*operands)


def dot(a, b, over_a, over_b):
    return lax.dot_general(a, b, (((over_a,), (over_b,)), ((), ())), preferred_element_type=F32)


def spread(block, axis, groups):
    count = len(groups[0])
    copies = jnp.broadcast_to(block[None], (count,) + block.shape)
    return lax.all_to_all(copies, axis, 0, 0, tiled=True, axis_index_groups=groups)


def pack_kernel(*refs):
    inputs, (down_right, up_left, send, keep, sem) = refs[:6], refs[6:]
    mine = 2 * lax.rem(lax.axis_index("par"), 2)
    copies = []
    for k in range(6):
        for first, to in ((2 - mine, send), (mine, keep)):
            copies.append((inputs[k].at[pl.ds(first, 2)], to.at[pl.ds(2 * k, 2)]))
    copies.append((up_left, send.at[pl.ds(12, 2)]))
    copies.append((down_right, send.at[pl.ds(14, 4)]))
    copies = [pltpu.make_async_copy(a, b, sem) for a, b in copies]
    for copy in copies:
        copy.start()
    for copy in copies:
        copy.wait()


def pack(inputs, down_right, up_left):
    return call(
        pack_kernel,
        [((18, 128, 128), BF), ((12, 128, 128), BF)],
        *inputs,
        down_right,
        up_left,
        specs=[HBM] * 8,
        scratch=[pltpu.SemaphoreType.DMA],
    )


def rows_of(keep, other, k):
    own = keep[2 * k : 2 * k + 2].reshape(256, 128)
    far = other[2 * k : 2 * k + 2].reshape(256, 128)
    return jnp.concatenate([own, far], axis=1)


def first_kernel(keep, down_right, up_left, other, part):
    def put(at, value):
        part[:, :, at : at + value.shape[1]] = value.astype(BF).reshape(16, 16, value.shape[1])

    weight = [jnp.concatenate([down_right[m], other[14 + m]], axis=0) for m in range(4)]
    hidden = rows_of(keep, other, 0)
    put(0, dot(hidden, jnp.concatenate(weight[:2], axis=1), 1, 0))
    put(256, dot(hidden, weight[2], 1, 0))
    put(384, dot(rows_of(keep, other, 1), weight[3], 1, 0))
    for half in range(2):
        weight = jnp.concatenate([up_left[half], other[12 + half]], axis=1)
        pair = [
            dot(rows_of(keep, other, 2 + 2 * half + i), weight[64 * i : 64 * i + 64], 1, 1)
            for i in range(2)
        ]
        put(512 + 128 * half, jnp.concatenate(pair, axis=1))


def first(keep, down_right, up_left, other):
    return call(first_kernel, [((16, 16, 768), BF)], keep, down_right, up_left, other)[0]


ORDER = (0, 1, 3, 2)


def side_kernel(near, next_y, far_y, factor, out):
    place = lax.axis_index("ex")
    start = [
        pl.multiple_of(16 * jnp.bitwise_xor(place, 4 * y + z), 16) for y in ORDER for z in ORDER
    ]
    for m in range(4):
        at = slice(16 * m, 16 * m + 16)
        ranks = jnp.concatenate(
            [b[:, at, :].reshape(-1, 128) for b in (near, next_y, far_y)], axis=0
        )
        rows = jnp.concatenate([factor[m, pl.ds(s, 16), :] for s in start], axis=0)
        side = dot(ranks, rows, 0, 0).astype(BF)
        out[m] = side[:, :128]
        out[4 + m // 2, :, 64 * (m % 2) : 64 * (m % 2) + 64] = side[:, 128:]


def side_weights(near, next_y, far_y, factor):
    return call(side_kernel, [((6, 128, 128), BF)], near, next_y, far_y, factor)[0]


def late_kernel(keep, other, side, side_other, x_part, g_part):
    for m in range(4):
        source = rows_of(keep, other, 0 if m < 3 else 1)
        weight = jnp.concatenate([side[m], side_other[m]], axis=0)
        x_part[m] = dot(weight, source, 0, 1).astype(BF)
    for half in range(2):
        weight = jnp.concatenate([side[4 + half], side_other[4 + half]], axis=0)
        for i in range(2):
            m = 2 * half + i
            value = dot(weight, rows_of(keep, other, 2 + m), 0, 1)
            g_part[m] = value[64 * i : 64 * i + 64].astype(BF)


def late(keep, other, side, side_other):
    return call(
        late_kernel, [((4, 128, 256), BF), ((4, 64, 256), BF)], keep, other, side, side_other
    )


def join_kernel(full, x_part, g_part, out):
    for e in range(2):
        at = slice(128 * e, 128 * e + 128)
        rows = full[8 * e : 8 * e + 8].reshape(128, 768)
        right = jnp.zeros((64, 128), F32)
        left = [jnp.zeros((128, 128), F32)] * 2
        for m in range(4):
            right += dot(g_part[m, :, at], rows[:, 128 * m : 128 * m + 128], 1, 0)
            both = rows[:, 512 + 128 * (m // 2) : 640 + 128 * (m // 2)]
            left[m % 2] += dot(x_part[m, :, at], both, 1, 0)
        total = right + left[0].T[:64] + left[1].T[64:]
        out[:, 2 * e : 2 * e + 2] = total.reshape(32, 2, 128)


def join(full, x_part, g_part):
    return call(join_kernel, [((32, 4, 128), F32)], full, x_part, g_part)[0]


def swap(block, step):
    return lax.ppermute(block, "ex", [(i, i ^ step) for i in range(16)])


def per_device(*args):
    inputs, (lora_a, lora_b, up_left, up_right, down_left, down_right) = args[:6], args[6:]

    shard = jnp.concatenate([lora_a, lora_b.transpose(0, 2, 1)], axis=1).reshape(64, 128)
    factor = jnp.concatenate(
        [
            jnp.pad(up_right.reshape(4, 16, 8, 128), ((0, 0), (0, 0), (0, 0), (0, 64))),
            jnp.pad(down_left.reshape(4, 16, 8, 64), ((0, 0), (0, 0), (0, 0), (128, 0))),
        ],
        axis=2,
    ).reshape(4, 256, 192)

    up_left = up_left.transpose(0, 2, 1).reshape(2, 128, 128)

    send, keep = pack(inputs, down_right, up_left)
    other = lax.ppermute(send, "par", PAIR)
    one = swap(shard[None], 1)
    part = first(keep, down_right, up_left, other)
    part, one = lax.optimization_barrier((part, one))
    pieces = lax.all_to_all(part, "par", 0, 0, tiled=True, axis_index_groups=CHIPS)
    two = jnp.concatenate([shard[None], one])
    near = jnp.concatenate([two, swap(two, 3)])
    next_y = swap(near, 4)
    total = jnp.sum(pieces.astype(F32), axis=0).astype(BF)
    total, near, next_y = lax.optimization_barrier((total, near, next_y))
    full = spread(total, "par", CHIPS)
    far_y = swap(jnp.concatenate([near, next_y]), 12)
    side = side_weights(near, next_y, far_y, factor)
    side_other = lax.ppermute(side, "par", PAIR)
    x_part, g_part = late(keep, other, side, side_other)
    out = join(full, x_part, g_part)

    out = lax.all_to_all(out, "par", 0, 0, tiled=True)
    out = jnp.sum(out.reshape(16, 4, 2, 128), axis=0) * (1.0 / 128)
    return out.reshape(4, 256)


def solution(mesh):
    in_specs = (P("ex", None, "par"),) * 6 + (
        P(None, "ex", "par"),
        P(None, "par", "ex"),
        P(None, "par", None),
        P(),
        P(),
        P(None, "par", None),
    )
    return jax.shard_map(
        per_device, mesh=mesh, in_specs=in_specs, out_specs=P("ex", "par"), check_vma=False
    )
```

time: 97.1 us -> 82.4 us (0.85)
  blocking collectives: 34.9 us -> 15.5 us
  starting transfers between devices: 29.8 us -> 47.6 us
  local copies, waits for them, and re-layouts: 11.7 us -> 1.52 us
  Pallas kernels: 0 us -> 3.68 us
  matrix products: 2.97 us -> 0 us
  waiting for transfers between devices: 15.4 us -> 13.2 us
    all_to_all x1 -> x0, blocking collectives: 21.1 us -> none  [spread(): lax.all_to_all(copies, axis, 0, 0, tiled=True, axis_index_groups=groups)]
    ppermute x1 -> x5, starting transfers between devices: 8.79 us -> 28.3 us  [the longest x4 19.5 us: swap(): return lax.ppermute(block, 'ex', [(i, i ^ step) for i in range(16)])]
    all_to_all x2 -> x1, waiting for transfers between devices: 12.7 us -> 0.01 us  [spread(): lax.all_to_all(copies, axis, 0, 0, tiled=True, axis_index_groups=groups)]
    ppermute x1 -> x5, waiting for transfers between devices: 0.01 us -> 12.1 us  [the longest x4 12.1 us: swap(): return lax.ppermute(block, 'ex', [(i, i ^ step) for i in range(16)])]
    unnamed x30 -> x14, local copies, waits for them, and re-layouts: 6.89 us -> 0.75 us
    pallas_call x0 -> x5, Pallas kernels: none -> 3.68 us  [call(): pl.pallas_call(kernel, out_shape=tuple((pltpu.VMEM(shape, dtype) for shap...]
    dot_general x15 -> x0, matrix products: 2.97 us -> none  [the longest x12 2.37 us: mm(): return jnp.dot(a, b, preferred_element_type=F32)]
    all_to_all x1, blocking collectives: 13.8 us -> 15.5 us  [per_device(): out = lax.all_to_all(out, 'par', 0, 0, tiled=True)]
  transfers between devices with their start and end apart: 5 -> 8, of which waited for: 4 -> 5; matrix products, arithmetic and copies ran while one was open for 6% -> 0% of each run, Pallas kernels for 0% -> 2%
where the time goes in v2:
time: 82.4 us; the launch traced here: 81.9 us
  starting transfers between devices  47.6 us (58%)
  blocking collectives  15.5 us (19%)
  waiting for transfers between devices  13.2 us (16%)
  Pallas kernels  3.68 us (4%)
  local copies, waits for them, and re-layouts  1.52 us (2%)
    ppermute x4, starting transfers between devices, swap(): return lax.ppermute(block, 'ex', [(i, i ^ step) for i in range(16)])  19.5 us
    all_to_all x1, blocking collectives, per_device(): out = lax.all_to_all(out, 'par', 0, 0, tiled=True)  15.5 us
    ppermute x4, waiting for transfers between devices, swap(): return lax.ppermute(block, 'ex', [(i, i ^ step) for i in range(16)])  12.1 us
    all_to_all x1, starting transfers between devices, spread(): lax.all_to_all(copies, axis, 0, 0, tiled=True, axis_index_groups=groups)  9.18 us
    ppermute x1, starting transfers between devices, per_device(): other = lax.ppermute(send, 'par', PAIR)  8.76 us
    ppermute x1, starting transfers between devices, per_device(): side_other = lax.ppermute(side, 'par', PAIR)  5.56 us
    all_to_all x1, starting transfers between devices, per_device(): lax.all_to_all(part, 'par', 0, 0, tiled=True, axis_index_groups=CHIPS)  4.51 us
    pallas_call x5, Pallas kernels, call(): pl.pallas_call(kernel, out_shape=tuple((pltpu.VMEM(shape, dtype) for shap...  3.68 us
  transfers between devices with their start and end apart: 8, of which 5 were waited for; matrix products, arithmetic and copies ran while one was open for 0% of the time, Pallas kernels for 2%

profile of v2, /device:TPU:1, one launch (start us, length us, event | category | flops | bytes accessed | tf_op | source)
XLA Modules:
  0.0 81.9 jit_solution(2338971960583908948)
XLA Ops:
  0.0 0.0 copy-start.4
  0.0 0.0 copy-start.5
  0.0 0.0 copy-start
  0.0 0.0 copy-start.1
  0.0 1.3 %pack_kernel.1 = (bf16[18,128,128]{2,1,0:T(8,128)(2,1)S(1)}, bf16[12,128,128]{2,1,0:T(8,128)(2,1)S(1)}) custom-call(bf16[4,128,128]{2,1,0:T(8,128)(2,1)} %refs_0_.1, bf16[4,128,128]{2,1,0:T(8,128)(2,1)} %refs_1_.1, bf16[4,128,128]{2,1,0:T(8,128)(2,1)} %refs_2_.1, bf16[4,128,128]{2,1,0:T(8,128)(2,1)} %refs_3_.1, bf16[4,128,128]{2,1,0:T(8,128)(2,1)} %refs_4_.1, ...), custom_call_target="tpu_custom_call" | custom-call | tf_op jit(solution)/shard_map/pack_kernel/pallas_call | solution.py:25
  1.4 8.8 %collective-permute-start = (bf16[18,128,128]{2,1,0:T(8,128)(2,1)S(1)}, bf16[18,128,128]{2,1,0:T(8,128)(2,1)S(1)}, u32[]{:S(2)}, u32[]{:S(2)}) collective-permute-start(bf16[18,128,128]{2,1,0:T(8,128)(2,1)S(1)} %get-tuple-element.15), channel_id=1, source_target_pairs={{0,1},{1,0},{2,3},{3,2},{4,5},{5,4},{6,7},{7,6},{8,9},{9,8},{10,11... | collective-permute-start | bytes 1769480 | tf_op jit(solution)/shard_map/ppermute | solution.py:180
  10.1 0.0 copy-done.4
  10.1 0.0 copy-done.5
  10.2 3.5 %collective-permute-start.1 = (bf16[1,64,128]{2,1,0:T(8,128)(2,1)S(1)}, bf16[1,64,128]{2,1,0:T(8,128)(2,1)S(1)}, u32[]{:S(2)}, u32[]{:S(2)}) collective-permute-start(bf16[1,64,128]{2,1,0:T(8,128)(2,1)S(1)} %bitcast.19), channel_id=1, source_target_pairs={{0,32},{32,0},{64,96},{96,64},{128,160},{160,128},{192,224},{224,1... | collective-permute-start | bytes 49160 | tf_op jit(solution)/shard_map/ppermute | solution.py:162
  13.6 0.0 collective-permute-done.other
  13.7 0.0 copy-done
  13.7 0.0 copy-done.1
  13.7 1.2 %first_kernel.1 = bf16[16,16,768]{2,1,0:T(8,128)(2,1)} custom-call(bf16[12,128,128]{2,1,0:T(8,128)(2,1)S(1)} %get-tuple-element.14.keep, bf16[4,128,128]{2,1,0:T(8,128)(2,1)S(1)} %copy-done, bf16[2,128,128]{2,1,0:T(8,128)(2,1)S(1)} %bitcast.16, bf16[18,128,128]{2,1,0:T(8,128)(2,1)S(1)} %collective-permute-done.other), custom_call_target="tpu_custom_call" | custom-call | tf_op jit(solution)/shard_map/first_kernel/pallas_call | solution.py:25
  14.9 3.7 %collective-permute-done.1 = bf16[1,64,128]{2,1,0:T(8,128)(2,1)S(1)} collective-permute-done((bf16[1,64,128]{2,1,0:T(8,128)(2,1)S(1)}, bf16[1,64,128]{2,1,0:T(8,128)(2,1)S(1)}, u32[]{:S(2)}, u32[]{:S(2)}) %collective-permute-start.1) | collective-permute-done | bytes 16416 | tf_op jit(solution)/shard_map/ppermute | solution.py:162
  18.6 4.5 %all-to-all-start = ((bf16[16,16,768]{2,1,0:T(8,128)(2,1)}), bf16[16,16,768]{2,1,0:T(8,128)(2,1)S(1)}, u32[]{:S(2)}, u32[]{:S(2)}) async-start(bf16[16,16,768]{2,1,0:T(8,128)(2,1)} %first_kernel.1), calls=%async_computation | async-start | bytes 786432 | tf_op jit(solution)/shard_map/all_to_all | solution.py:184
  23.1 8.1 %collective-permute-start.2 = (bf16[2,64,128]{2,1,0:T(8,128)(2,1)S(1)}, bf16[2,64,128]{2,1,0:T(8,128)(2,1)S(1)}, u32[]{:S(2)}, u32[]{:S(2)}) collective-permute-start(bf16[2,64,128]{2,1,0:T(8,128)(2,1)S(1)} %pad_maximum_fusion.2), channel_id=1, source_target_pairs={{0,96},{32,64},{64,32},{96,0},{128,224},{160,192},{192,160},{224,1... | collective-permute-start | bytes 98312 | tf_op jit(solution)/shard_map/ppermute | solution.py:162
  31.2 4.3 %collective-permute-done.2 = bf16[2,64,128]{2,1,0:T(8,128)(2,1)S(1)} collective-permute-done((bf16[2,64,128]{2,1,0:T(8,128)(2,1)S(1)}, bf16[2,64,128]{2,1,0:T(8,128)(2,1)S(1)}, u32[]{:S(2)}, u32[]{:S(2)}) %collective-permute-start.2) | collective-permute-done | bytes 32800 | tf_op jit(solution)/shard_map/ppermute | solution.py:162
  35.5 3.2 %collective-permute-start.3 = (bf16[4,64,128]{2,1,0:T(8,128)(2,1)S(1)}, bf16[4,64,128]{2,1,0:T(8,128)(2,1)S(1)}, u32[]{:S(2)}, u32[]{:S(2)}) collective-permute-start(bf16[4,64,128]{2,1,0:T(8,128)(2,1)S(1)} %pad_maximum_fusion.1.near), channel_id=1, source_target_pairs={{0,128},{32,160},{64,192},{96,224},{128,0},{160,32},{192,64},{224,... | collective-permute-start | bytes 196616 | tf_op jit(solution)/shard_map/ppermute | solution.py:162
  38.7 0.0 all-to-all-done
  38.7 0.1 reduce_sum.21
  38.8 1.7 %collective-permute-done.3.next_y = bf16[4,64,128]{2,1,0:T(8,128)(2,1)S(1)} collective-permute-done((bf16[4,64,128]{2,1,0:T(8,128)(2,1)S(1)}, bf16[4,64,128]{2,1,0:T(8,128)(2,1)S(1)}, u32[]{:S(2)}, u32[]{:S(2)}) %collective-permute-start.3) | collective-permute-done | bytes 65568 | tf_op jit(solution)/shard_map/ppermute | solution.py:162
  40.5 0.8 broadcast_in_dim.2
  41.3 9.2 %all-to-all-start.1 = ((bf16[16,16,768]{2,1,0:T(8,128)(2,1)}), bf16[16,16,768]{2,1,0:T(8,128)(2,1)S(1)}, u32[]{:S(2)}, u32[]{:S(2)}) async-start(bf16[16,16,768]{2,1,0:T(8,128)(2,1)} %broadcast_in_dim.2), calls=%async_computation.1 | async-start | bytes 786432 | tf_op jit(solution)/shard_map/all_to_all | solution.py:42
  50.5 0.0 copy-start.3
  50.5 0.0 copy-start.2
  50.5 4.8 %collective-permute-start.4 = (bf16[8,64,128]{2,1,0:T(8,128)(2,1)S(1)}, bf16[8,64,128]{2,1,0:T(8,128)(2,1)S(1)}, u32[]{:S(2)}, u32[]{:S(2)}) collective-permute-start(bf16[8,64,128]{2,1,0:T(8,128)(2,1)S(1)} %pad_maximum_fusion), channel_id=1, source_target_pairs={{0,384},{32,416},{64,448},{96,480},{128,256},{160,288},{192,320},{... | collective-permute-start | bytes 393224 | tf_op jit(solution)/shard_map/ppermute | solution.py:162
  55.3 0.0 copy-done.3
  55.3 0.1 copy.14
  55.5 0.0 copy-done.2
  55.5 2.4 %collective-permute-done.4.far_y = bf16[8,64,128]{2,1,0:T(8,128)(2,1)S(1)} collective-permute-done((bf16[8,64,128]{2,1,0:T(8,128)(2,1)S(1)}, bf16[8,64,128]{2,1,0:T(8,128)(2,1)S(1)}, u32[]{:S(2)}, u32[]{:S(2)}) %collective-permute-start.4) | collective-permute-done | bytes 131104 | tf_op jit(solution)/shard_map/ppermute | solution.py:162
  57.9 0.3 side_kernel.1.side
  58.3 5.6 %collective-permute-start.5 = (bf16[6,128,128]{2,1,0:T(8,128)(2,1)S(1)}, bf16[6,128,128]{2,1,0:T(8,128)(2,1)S(1)}, u32[]{:S(2)}, u32[]{:S(2)}) collective-permute-start(bf16[6,128,128]{2,1,0:T(8,128)(2,1)S(1)} %side_kernel.1.side), channel_id=1, source_target_pairs={{0,1},{1,0},{2,3},{3,2},{4,5},{5,4},{6,7},{7,6},{8,9},{9,8},{10,11... | collective-permute-start | bytes 589832 | tf_op jit(solution)/shard_map/ppermute | solution.py:193
  63.8 1.0 %collective-permute-done.5.side_other = bf16[6,128,128]{2,1,0:T(8,128)(2,1)S(1)} collective-permute-done((bf16[6,128,128]{2,1,0:T(8,128)(2,1)S(1)}, bf16[6,128,128]{2,1,0:T(8,128)(2,1)S(1)}, u32[]{:S(2)}, u32[]{:S(2)}) %collective-permute-start.5) | collective-permute-done | bytes 196640 | tf_op jit(solution)/shard_map/ppermute | solution.py:193
  64.9 0.5 late_kernel.1
  65.4 0.0 all-to-all-done.1.full
  65.4 0.4 join_kernel.1
  65.7 15.5 %all_to_all.15 = f32[32,4,128]{2,1,0:T(4,128)S(1)} all-to-all(f32[32,4,128]{2,1,0:T(4,128)S(1)} %join_kernel.1), channel_id=1, replica_groups=mesh['ex'=16,'par'=32] {'par'}, dimensions={0} | all-to-all | bytes 131072 | tf_op jit(solution)/shard_map/all_to_all | solution.py:197
  81.3 0.6 copy.17
  (7 shorter events, 0.1 us)
Async XLA Ops:
  0.0 10.1 %copy-start.4 = (bf16[4,128,8]{1,2,0:T(8,128)(2,1)S(1)}, bf16[4,128,8]{1,2,0:T(8,128)(2,1)}, u32[]{:S(2)}) copy-start(bf16[4,128,8]{1,2,0:T(8,128)(2,1)} %param.19) | copy-start | bytes 24580
  0.0 10.1 %copy-start.5 = (bf16[4,8,128]{2,1,0:T(8,128)(2,1)S(1)}, bf16[4,8,128]{2,1,0:T(8,128)(2,1)}, u32[]{:S(2)}) copy-start(bf16[4,8,128]{2,1,0:T(8,128)(2,1)} %param.18) | copy-start | bytes 24580
  0.0 13.7 %copy-start = (bf16[4,128,128]{2,1,0:T(8,128)(2,1)S(1)}, bf16[4,128,128]{2,1,0:T(8,128)(2,1)}, u32[]{:S(2)}) copy-start(bf16[4,128,128]{2,1,0:T(8,128)(2,1)} %down_right.1) | copy-start | bytes 393220
  0.0 13.7 %copy-start.1 = (bf16[4,128,64]{1,2,0:T(8,128)(2,1)S(1)}, bf16[4,128,64]{1,2,0:T(8,128)(2,1)}, u32[]{:S(2)}) copy-start(bf16[4,128,64]{1,2,0:T(8,128)(2,1)} %param.20) | copy-start | bytes 196612
  1.4 12.3 %collective-permute-start = (bf16[18,128,128]{2,1,0:T(8,128)(2,1)S(1)}, bf16[18,128,128]{2,1,0:T(8,128)(2,1)S(1)}, u32[]{:S(2)}, u32[]{:S(2)}) collective-permute-start(bf16[18,128,128]{2,1,0:T(8,128)(2,1)S(1)} %get-tuple-element.15), channel_id=1, source_target_pairs={{0,1},{1,0},{2,3},{3,2},{4,5},{5,4},{6,7},{7,6},{8,9},{9,8},{10,11... | collective-permute-start | bytes 1769480 | tf_op jit(solution)/shard_map/ppermute | solution.py:180
  10.2 8.4 %collective-permute-start.1 = (bf16[1,64,128]{2,1,0:T(8,128)(2,1)S(1)}, bf16[1,64,128]{2,1,0:T(8,128)(2,1)S(1)}, u32[]{:S(2)}, u32[]{:S(2)}) collective-permute-start(bf16[1,64,128]{2,1,0:T(8,128)(2,1)S(1)} %bitcast.19), channel_id=1, source_target_pairs={{0,32},{32,0},{64,96},{96,64},{128,160},{160,128},{192,224},{224,1... | collective-permute-start | bytes 49160 | tf_op jit(solution)/shard_map/ppermute | solution.py:162
  18.6 20.2 %all-to-all-start = ((bf16[16,16,768]{2,1,0:T(8,128)(2,1)}), bf16[16,16,768]{2,1,0:T(8,128)(2,1)S(1)}, u32[]{:S(2)}, u32[]{:S(2)}) async-start(bf16[16,16,768]{2,1,0:T(8,128)(2,1)} %first_kernel.1), calls=%async_computation | async-start | bytes 786432 | tf_op jit(solution)/shard_map/all_to_all | solution.py:184
  23.1 12.4 %collective-permute-start.2 = (bf16[2,64,128]{2,1,0:T(8,128)(2,1)S(1)}, bf16[2,64,128]{2,1,0:T(8,128)(2,1)S(1)}, u32[]{:S(2)}, u32[]{:S(2)}) collective-permute-start(bf16[2,64,128]{2,1,0:T(8,128)(2,1)S(1)} %pad_maximum_fusion.2), channel_id=1, source_target_pairs={{0,96},{32,64},{64,32},{96,0},{128,224},{160,192},{192,160},{224,1... | collective-permute-start | bytes 98312 | tf_op jit(solution)/shard_map/ppermute | solution.py:162
  35.5 5.0 %collective-permute-start.3 = (bf16[4,64,128]{2,1,0:T(8,128)(2,1)S(1)}, bf16[4,64,128]{2,1,0:T(8,128)(2,1)S(1)}, u32[]{:S(2)}, u32[]{:S(2)}) collective-permute-start(bf16[4,64,128]{2,1,0:T(8,128)(2,1)S(1)} %pad_maximum_fusion.1.near), channel_id=1, source_target_pairs={{0,128},{32,160},{64,192},{96,224},{128,0},{160,32},{192,64},{224,... | collective-permute-start | bytes 196616 | tf_op jit(solution)/shard_map/ppermute | solution.py:162
  41.3 24.1 %all-to-all-start.1 = ((bf16[16,16,768]{2,1,0:T(8,128)(2,1)}), bf16[16,16,768]{2,1,0:T(8,128)(2,1)S(1)}, u32[]{:S(2)}, u32[]{:S(2)}) async-start(bf16[16,16,768]{2,1,0:T(8,128)(2,1)} %broadcast_in_dim.2), calls=%async_computation.1 | async-start | bytes 786432 | tf_op jit(solution)/shard_map/all_to_all | solution.py:42
  50.5 4.8 %copy-start.3 = (bf16[4,128,64]{1,2,0:T(8,128)(2,1)S(1)}, bf16[4,128,64]{1,2,0:T(8,128)(2,1)}, u32[]{:S(2)}) copy-start(bf16[4,128,64]{1,2,0:T(8,128)(2,1)} %param.22) | copy-start | bytes 196612
  50.5 4.9 %copy-start.2 = (bf16[4,128,128]{2,1,0:T(8,128)(2,1)S(1)}, bf16[4,128,128]{2,1,0:T(8,128)(2,1)}, u32[]{:S(2)}) copy-start(bf16[4,128,128]{2,1,0:T(8,128)(2,1)} %param.21) | copy-start | bytes 393220
  50.5 7.4 %collective-permute-start.4 = (bf16[8,64,128]{2,1,0:T(8,128)(2,1)S(1)}, bf16[8,64,128]{2,1,0:T(8,128)(2,1)S(1)}, u32[]{:S(2)}, u32[]{:S(2)}) collective-permute-start(bf16[8,64,128]{2,1,0:T(8,128)(2,1)S(1)} %pad_maximum_fusion), channel_id=1, source_target_pairs={{0,384},{32,416},{64,448},{96,480},{128,256},{160,288},{192,320},{... | collective-permute-start | bytes 393224 | tf_op jit(solution)/shard_map/ppermute | solution.py:162
  58.3 6.6 %collective-permute-start.5 = (bf16[6,128,128]{2,1,0:T(8,128)(2,1)S(1)}, bf16[6,128,128]{2,1,0:T(8,128)(2,1)S(1)}, u32[]{:S(2)}, u32[]{:S(2)}) collective-permute-start(bf16[6,128,128]{2,1,0:T(8,128)(2,1)S(1)} %side_kernel.1.side), channel_id=1, source_target_pairs={{0,1},{1,0},{2,3},{3,2},{4,5},{5,4},{6,7},{7,6},{8,9},{9,8},{10,11... | collective-permute-start | bytes 589832 | tf_op jit(solution)/shard_map/ppermute | solution.py:193

commit v3 on v2

v3 whole, which is shorter than its diff:
```python
import jax
import jax.numpy as jnp
from jax import lax
from jax.experimental import pallas as pl
from jax.experimental.pallas import tpu as pltpu
from jax.sharding import PartitionSpec as P

BF = jnp.bfloat16
F32 = jnp.float32

Z_HI = [[4 * y + z for z in range(4)] for y in range(4)]
Y = [[4 * y + z for y in range(4)] for z in range(4)]
CHIPS = [[2 * chip + core for chip in range(16)] for core in range(2)]
PAIR = [(i, i ^ 1) for i in range(32)]
CHAIN = 0
VMEM = pl.BlockSpec(memory_space=pltpu.VMEM)
HBM = pl.BlockSpec(memory_space=pl.ANY)
LOOSE = pl.BlockSpec(memory_space=pltpu.VMEM)


def call(kernel, outs, *operands, specs=None, scratch=(), place=pltpu.VMEM):
    specs = specs or [VMEM] * len(operands)
    operands = [
        pltpu.with_memory_space_constraint(a, pltpu.VMEM) if spec is VMEM else a
        for a, spec in zip(operands, specs)
    ]
    return pl.pallas_call(
        kernel,
        out_shape=tuple(place(shape, dtype) for shape, dtype in outs),
        in_specs=specs,
        out_specs=(VMEM,) * len(outs),
        scratch_shapes=scratch,
        name=kernel.__name__,
    )(*operands)


def dot(a, b, over_a, over_b):
    return lax.dot_general(a, b, (((over_a,), (over_b,)), ((), ())), preferred_element_type=F32)


def spread(block, axis, groups):
    count = len(groups[0])
    copies = jnp.broadcast_to(block[None], (count,) + block.shape)
    return lax.all_to_all(copies, axis, 0, 0, tiled=True, axis_index_groups=groups)


UL, DR, RANKS, ALL = 3072, 3328, 3840, 3904


def pack_kernel(*refs):
    inputs, (down_right, up_left, lora_a, lora_b, send, ranks, sem) = refs[:6], refs[6:]
    copies = [(lora_a, ranks.at[0]), (lora_b, ranks.at[1])]
    copies += [(inputs[k], send.at[pl.ds(512 * k, 512)]) for k in range(6)]
    copies.append((up_left, send.at[pl.ds(UL, 256)]))
    copies.append((down_right, send.at[pl.ds(DR, 512)]))
    copies = [pltpu.make_async_copy(a, b, sem) for a, b in copies]
    for copy in copies:
        copy.start()
    for copy in copies:
        copy.wait()
    a, b = ranks[0].astype(F32), ranks[1].astype(F32)
    parts = [v[8 * m : 8 * m + 8] for m in range(4) for v in (a, b)]
    send[RANKS:ALL] = jnp.concatenate(parts, axis=0).astype(BF)


def pack(inputs, down_right, up_left, lora_a, lora_b):
    return call(
        pack_kernel,
        [((ALL, 128), BF)],
        *[a.reshape(512, 128) for a in inputs],
        down_right.reshape(512, 128),
        up_left.transpose(0, 2, 1).reshape(256, 128),
        lora_a.reshape(32, 128),
        lora_b.transpose(0, 2, 1).reshape(32, 128),
        specs=[HBM] * 10,
        scratch=[pltpu.VMEM((2, 32, 128), BF), pltpu.SemaphoreType.DMA],
    )[0]


def rows_of(own, other, k):
    at = slice(512 * k, 512 * k + 512)
    return jnp.concatenate([own[at], other[at]], axis=1)


def first_kernel(own, other, part, ranks, far):
    role = lax.rem(lax.axis_index("par") + CHAIN, 2)
    start = pl.multiple_of(256 * role, 256)
    ranks[:64] = own[RANKS:ALL]
    ranks[64:] = other[RANKS:ALL]
    for k in range(6):
        at = slice(256 * k, 256 * k + 256)
        far[at] = other[pl.ds(512 * k + start, 256)]

    def put(at, value):
        part[:, :, at : at + value.shape[1]] = value.astype(BF).reshape(16, 32, value.shape[1])

    def right(m):
        at = slice(DR + 128 * m, DR + 128 * m + 128)
        return jnp.concatenate([own[at], other[at]], axis=0)

    @pl.when(role == 0)
    def _():
        hidden = rows_of(own, other, 0)
        put(0, dot(hidden, jnp.concatenate([right(0), right(1)], axis=1), 1, 0))
        put(256, dot(hidden, right(2), 1, 0))
        put(384, dot(rows_of(own, other, 1), right(3), 1, 0))
        left = jnp.concatenate([own[UL:DR], other[UL:DR]], axis=1)
        for half in range(2):
            pair = [
                dot(rows_of(own, other, 2 + m), left[64 * m : 64 * m + 64], 1, 1)
                for m in (2 * half, 2 * half + 1)
            ]
            put(512 + 128 * half, jnp.concatenate(pair, axis=1))

    @pl.when(role == 1)
    def _():
        part[...] = jnp.zeros_like(part)


def first(own, other):
    rows = ((UL // 2, 128), BF)
    shapes = [((16, 32, 768), BF), ((128, 128), BF), rows]
    return call(first_kernel, shapes, own, other, place=jax.ShapeDtypeStruct)


def side_kernel(gathered, factor, out):
    for m in range(4):
        for core in range(2):
            at = slice(64 * core + 16 * m, 64 * core + 16 * m + 16)
            ranks = gathered[:, at, :].reshape(256, 128)
            side = dot(ranks, factor[m], 0, 0).astype(BF)
            rows = slice(128 - 128 * core, 256 - 128 * core)
            out[rows, 128 * m : 128 * m + 128] = side[:, :128]
            out[rows, 512 + 64 * m : 576 + 64 * m] = side[:, 128:]
    out[256:] = jnp.zeros((256, 768), BF)


def load_kernel(*refs):
    inputs, (other, mine, far, sem) = refs[:6], refs[6:]
    role = lax.rem(lax.axis_index("par") + CHAIN, 2)
    rows = pl.ds(pl.multiple_of(256 * role, 256), 256)
    copies = [(inputs[k].at[rows], mine.at[pl.ds(256 * k, 256)]) for k in range(6)]
    copies.append((other, far))
    copies = [pltpu.make_async_copy(a, b, sem) for a, b in copies]
    for copy in copies:
        copy.start()
    for copy in copies:
        copy.wait()


def load(inputs, other):
    shape = ((1536, 128), BF)
    return call(
        load_kernel,
        [shape, shape],
        *[a.reshape(512, 128) for a in inputs],
        other,
        specs=[HBM] * 7,
        scratch=[pltpu.SemaphoreType.DMA],
    )


def finish_kernel(have, got, *refs):
    inputs, (other, out, mine, far, sem) = refs[:6], refs[6:]
    role = lax.rem(lax.axis_index("par") + CHAIN, 2)
    rows = pl.ds(pl.multiple_of(256 * role, 256), 256)
    copies = [(inputs[k].at[rows], mine.at[pl.ds(256 * k, 256)]) for k in range(6)]
    copies.append((other, far))
    copies = [pltpu.make_async_copy(a, b, sem) for a, b in copies]
    for copy in copies:
        copy.start()
    for copy in copies:
        copy.wait()

    def add_up(full, side, first, own, other):
        def rows(k):
            at = slice(256 * k, 256 * k + 256)
            return jnp.concatenate([own[at], other[at]], axis=1)

        hidden = rows(0)
        x_left = [dot(hidden, side[:256, 128 * m : 128 * m + 128], 1, 0) for m in range(3)]
        x_left.append(dot(rows(1), side[:256, 384:512], 1, 0))
        g_right = [dot(rows(2 + m), side[:256, 512 + 64 * m : 576 + 64 * m], 1, 0) for m in range(4)]
        x_left = [x.astype(BF) for x in x_left]
        g_right = [g.astype(BF) for g in g_right]
        for e in range(2):
            at, here = slice(128 * e, 128 * e + 128), slice(first + 128 * e, first + 128 * e + 128)
            total = jnp.zeros((64, 128), F32)
            for m in range(4):
                x, g = slice(128 * m, 128 * m + 128), slice(512 + 64 * m, 576 + 64 * m)
                total += dot(full[here, g], x_left[m][at], 0, 0)
                total += dot(g_right[m][at], full[here, x], 0, 0)
            out[:, 2 * e : 2 * e + 2] = total.reshape(32, 2, 128)

    mover = lax.rem(lax.axis_index("par"), 2) == CHAIN

    @pl.when(mover)
    def _():
        add_up(have, got, 0, mine, far)

    @pl.when(jnp.logical_not(mover))
    def _():
        add_up(got, have, 256, far, mine)


def move_rows(part, ranks, factor):
    pieces = lax.all_to_all(part, "par", 0, 0, tiled=True, axis_index_groups=CHIPS)
    total = jnp.sum(pieces.astype(F32), axis=0).astype(BF)
    return spread(total, "par", CHIPS).reshape(512, 768)


def gather_ranks(part, ranks, factor):
    along_z = spread(ranks, "ex", Z_HI).reshape(512, 128)
    gathered = spread(along_z, "ex", Y).reshape(16, 128, 128)
    return call(side_kernel, [((512, 768), BF)], gathered, factor, specs=[VMEM, LOOSE])[0]


def per_device(*args):
    inputs, (lora_a, lora_b, up_left, up_right, down_left, down_right) = args[:6], args[6:]

    factor = jnp.concatenate(
        [
            jnp.pad(up_right.reshape(4, 16, 8, 128), ((0, 0), (0, 0), (0, 0), (0, 64))),
            jnp.pad(down_left.reshape(4, 16, 8, 64), ((0, 0), (0, 0), (0, 0), (128, 0))),
        ],
        axis=2,
    ).reshape(4, 256, 192)

    own = pack(inputs, down_right, up_left, lora_a, lora_b)
    other = lax.ppermute(own, "par", PAIR)
    part, ranks, far = first(own, other)
    mover = lax.axis_index("par") % 2 == CHAIN
    have = lax.cond(mover, move_rows, gather_ranks, part, ranks, factor)
    got = lax.ppermute(have, "par", PAIR)
    out = call(finish_kernel, [((32, 4, 128), F32)], have, got, *[a.reshape(512, 128) for a in inputs], far, specs=[VMEM, VMEM] + [HBM] * 7, scratch=[pltpu.VMEM((1536, 128), BF), pltpu.VMEM((1536, 128), BF), pltpu.SemaphoreType.DMA])[0]
    out = lax.all_to_all(out, "par", 0, 0, tiled=True)
    out = jnp.sum(out.reshape(16, 4, 2, 128), axis=0) * (1.0 / 128)
    return out.reshape(4, 256)


def solution(mesh):
    in_specs = (P("ex", None, "par"),) * 6 + (
        P(None, "ex", "par"),
        P(None, "par", "ex"),
        P(None, "par", None),
        P(),
        P(),
        P(None, "par", None),
    )
    return jax.shard_map(
        per_device, mesh=mesh, in_specs=in_specs, out_specs=P("ex", "par"), check_vma=False
    )
```

time: 82.4 us -> 70 us (0.85)
  starting transfers between devices: 47.6 us -> 14.9 us
  blocking collectives: 15.5 us -> 45.3 us
  waiting for transfers between devices: 13.2 us -> 3.86 us
    all_to_all x0 -> x2, blocking collectives: none -> 34.1 us  [spread(): lax.all_to_all(copies, axis, 0, 0, tiled=True, axis_index_groups=groups)]
    ppermute x6 -> x2, starting transfers between devices: 33.9 us -> 14.9 us  [the longest x1 8.92 us: per_device(): other = lax.ppermute(own, 'par', PAIR)]
    all_to_all x2 -> x0, starting transfers between devices: 13.7 us -> none  [the longest x1 9.18 us: spread(): lax.all_to_all(copies, axis, 0, 0, tiled=True, axis_index_groups=groups)]
    ppermute x6 -> x2, waiting for transfers between devices: 13.2 us -> 3.86 us  [the longest x1 1.97 us: per_device(): other = lax.ppermute(own, 'par', PAIR)]
    all_to_all x1, blocking collectives: 15.5 us -> 11.2 us  [per_device(): out = lax.all_to_all(out, 'par', 0, 0, tiled=True)]
    pallas_call x5 -> x4, Pallas kernels: 3.68 us -> 4.42 us  [call(): pl.pallas_call(kernel, out_shape=tuple((place(shape, dtype) for shape, dt...]
  transfers between devices with their start and end apart: 8 -> 2, of which waited for: 5 -> 2; matrix products, arithmetic and copies ran while one was open for 0% -> 0% of each run, Pallas kernels for 2% -> 0%
where the time goes in v3:
time: 70 us; the launch traced here: 69.5 us
  blocking collectives  45.3 us (65%)
  starting transfers between devices  14.9 us (21%)
  Pallas kernels  4.42 us (6%)
  waiting for transfers between devices  3.86 us (6%)
  local copies, waits for them, and re-layouts  0.82 us (1%)
    all_to_all x2, blocking collectives, spread(): lax.all_to_all(copies, axis, 0, 0, tiled=True, axis_index_groups=groups)  34.1 us
    all_to_all x1, blocking collectives, per_device(): out = lax.all_to_all(out, 'par', 0, 0, tiled=True)  11.2 us
    ppermute x1, starting transfers between devices, per_device(): other = lax.ppermute(own, 'par', PAIR)  8.92 us
    ppermute x1, starting transfers between devices, per_device(): got = lax.ppermute(have, 'par', PAIR)  5.97 us
    pallas_call x4, Pallas kernels, call(): pl.pallas_call(kernel, out_shape=tuple((place(shape, dtype) for shape, dt...  4.42 us
    ppermute x1, waiting for transfers between devices, per_device(): other = lax.ppermute(own, 'par', PAIR)  1.97 us
    ppermute x1, waiting for transfers between devices, per_device(): got = lax.ppermute(have, 'par', PAIR)  1.89 us
  transfers between devices with their start and end apart: 2, of which 2 were waited for; matrix products, arithmetic and copies ran while one was open for 0% of the time, Pallas kernels for 0%

profile of v3, /device:TPU:1, one launch (start us, length us, event | category | flops | bytes accessed | tf_op | source)
XLA Modules:
  0.0 69.5 jit_solution(10347563493425281333)
XLA Ops:
  0.0 0.0 copy-start.1
  0.0 1.3 %pack_kernel.1.own = bf16[3904,128]{1,0:T(8,128)(2,1)S(1)} custom-call(bf16[512,128]{1,0:T(8,128)(2,1)} %bitcast.31, bf16[512,128]{1,0:T(8,128)(2,1)} %bitcast.33, bf16[512,128]{1,0:T(8,128)(2,1)} %bitcast.35, bf16[512,128]{1,0:T(8,128)(2,1)} %bitcast.37, bf16[512,128]{1,0:T(8,128)(2,1)} %bitcast.39, bf16[512,128]{1,0:T(8,128)(2,1)} %bitcast.41, ...), custom_call_target="tpu_custom_call" | custom-call | tf_op jit(solution)/shard_map/pack_kernel/pallas_call | solution.py:27
  1.3 0.0 copy-start
  1.3 8.9 %collective-permute-start = (bf16[3904,128]{1,0:T(8,128)(2,1)S(1)}, bf16[3904,128]{1,0:T(8,128)(2,1)S(1)}, u32[]{:S(2)}, u32[]{:S(2)}) collective-permute-start(bf16[3904,128]{1,0:T(8,128)(2,1)S(1)} %pack_kernel.1.own), channel_id=1, source_target_pairs={{0,1},{1,0},{2,3},{3,2},{4,5},{5,4},{6,7},{7,6},{8,9},{9,8},{10,11... | collective-permute-start | bytes 2998280 | tf_op jit(solution)/shard_map/ppermute | solution.py:230
  10.3 0.0 copy-done.1
  10.3 0.1 copy.13
  10.4 0.0 copy-done
  10.5 2.0 %collective-permute-done.other = bf16[3904,128]{1,0:T(8,128)(2,1)S(1)} collective-permute-done((bf16[3904,128]{1,0:T(8,128)(2,1)S(1)}, bf16[3904,128]{1,0:T(8,128)(2,1)S(1)}, u32[]{:S(2)}, u32[]{:S(2)}) %collective-permute-start) | collective-permute-done | bytes 999456 | tf_op jit(solution)/shard_map/ppermute | solution.py:230
  12.5 0.8 %first_kernel.1 = (bf16[16,32,768]{2,1,0:T(8,128)(2,1)S(1)}, bf16[128,128]{1,0:T(8,128)(2,1)S(1)}, bf16[1536,128]{1,0:T(8,128)(2,1)}) custom-call(bf16[3904,128]{1,0:T(8,128)(2,1)S(1)} %pack_kernel.1.own, bf16[3904,128]{1,0:T(8,128)(2,1)S(1)} %collective-permute-done.other), custom_call_target="tpu_custom_call" | custom-call | tf_op jit(solution)/shard_map/first_kernel/pallas_call | solution.py:27
  13.3 34.6 %conditional.1 = (bf16[512,768]{1,0:T(8,128)(2,1)S(1)}) conditional(s32[]{:T(128)} %convert_element_type.6, (bf16[128,128]{1,0:T(8,128)(2,1)S(1)}, bf16[4,16,16,192]{3,2,1,0:T(8,128)(2,1)S(1)}) %tuple.11, bf16[16,32,768]{2,1,0:T(8,128)(2,1)S(1)} %get-tuple-element.20), branch_computations={%region_0.1_spmd, %region_1.3_spmd} | conditional | flops 368640 | bytes 4816906 | solution.py:233
  13.3 23.2 %all_to_all.21 = bf16[4,128,128]{2,1,0:T(8,128)(2,1)S(1)} all-to-all(bf16[4,128,128]{2,1,0:T(8,128)(2,1)S(1)} %broadcast_in_dim.1), channel_id=1, replica_groups={{0,32,64,96},{128,160,192,224},{256,288,320,352},{384,416,448,480},{1,3..., dimensions={0} | all-to-all | bytes 262144 | tf_op jit(solution)/shard_map/cond/branch_0_fun/all_to_all | solution.py:44
  36.5 0.1 broadcast_in_dim.6
  36.6 10.9 %all_to_all.22 = bf16[4,512,128]{2,1,0:T(8,128)(2,1)S(1)} all-to-all(bf16[4,512,128]{2,1,0:T(8,128)(2,1)S(1)} %broadcast_in_dim.6), channel_id=1, replica_groups={{0,128,256,384},{32,160,288,416},{64,192,320,448},{96,224,352,480},{1,1..., dimensions={0} | all-to-all | bytes 1048576 | tf_op jit(solution)/shard_map/cond/branch_0_fun/all_to_all | solution.py:44
  47.5 0.4 side_kernel.1
  47.9 6.0 %collective-permute-start.1 = (bf16[512,768]{1,0:T(8,128)(2,1)S(1)}, bf16[512,768]{1,0:T(8,128)(2,1)S(1)}, u32[]{:S(2)}, u32[]{:S(2)}) collective-permute-start(bf16[512,768]{1,0:T(8,128)(2,1)S(1)} %get-tuple-element.22.have), channel_id=1, source_target_pairs={{0,1},{1,0},{2,3},{3,2},{4,5},{5,4},{6,7},{7,6},{8,9},{9,8},{10,11... | collective-permute-start | bytes 2359304 | tf_op jit(solution)/shard_map/ppermute | solution.py:234
  53.9 1.9 %collective-permute-done.1.got = bf16[512,768]{1,0:T(8,128)(2,1)S(1)} collective-permute-done((bf16[512,768]{1,0:T(8,128)(2,1)S(1)}, bf16[512,768]{1,0:T(8,128)(2,1)S(1)}, u32[]{:S(2)}, u32[]{:S(2)}) %collective-permute-start.1) | collective-permute-done | bytes 786464 | tf_op jit(solution)/shard_map/ppermute | solution.py:234
  55.8 1.8 %finish_kernel.1 = f32[32,4,128]{2,1,0:T(4,128)S(1)} custom-call(bf16[512,768]{1,0:T(8,128)(2,1)S(1)} %get-tuple-element.22.have, bf16[512,768]{1,0:T(8,128)(2,1)S(1)} %collective-permute-done.1.got, bf16[512,128]{1,0:T(8,128)(2,1)} %bitcast.32, bf16[512,128]{1,0:T(8,128)(2,1)} %bitcast.34, bf16[512,128]{1,0:T(8,128)(2,1)} %bitcast.36, ...), custom_call_target="tpu_custom_call" | custom-call | tf_op jit(solution)/shard_map/finish_kernel/pallas_call | solution.py:27
  57.7 11.2 %all_to_all.25 = f32[32,4,128]{2,1,0:T(4,128)S(1)} all-to-all(f32[32,4,128]{2,1,0:T(4,128)S(1)} %finish_kernel.1), channel_id=1, replica_groups=mesh['ex'=16,'par'=32] {'par'}, dimensions={0} | all-to-all | bytes 131072 | tf_op jit(solution)/shard_map/all_to_all | solution.py:236
  68.9 0.6 copy.16
  (4 shorter events, 0.1 us)
Async XLA Ops:
  0.0 10.3 %copy-start.1 = (bf16[4,128,64]{1,2,0:T(8,128)(2,1)S(1)}, bf16[4,128,64]{1,2,0:T(8,128)(2,1)}, u32[]{:S(2)}) copy-start(bf16[4,128,64]{1,2,0:T(8,128)(2,1)} %param.24) | copy-start | bytes 196612
  1.3 9.1 %copy-start = (bf16[4,128,128]{2,1,0:T(8,128)(2,1)S(1)}, bf16[4,128,128]{2,1,0:T(8,128)(2,1)}, u32[]{:S(2)}) copy-start(bf16[4,128,128]{2,1,0:T(8,128)(2,1)} %param.23) | copy-start | bytes 393220
  1.3 11.1 %collective-permute-start = (bf16[3904,128]{1,0:T(8,128)(2,1)S(1)}, bf16[3904,128]{1,0:T(8,128)(2,1)S(1)}, u32[]{:S(2)}, u32[]{:S(2)}) collective-permute-start(bf16[3904,128]{1,0:T(8,128)(2,1)S(1)} %pack_kernel.1.own), channel_id=1, source_target_pairs={{0,1},{1,0},{2,3},{3,2},{4,5},{5,4},{6,7},{7,6},{8,9},{9,8},{10,11... | collective-permute-start | bytes 2998280 | tf_op jit(solution)/shard_map/ppermute | solution.py:230
  47.9 7.9 %collective-permute-start.1 = (bf16[512,768]{1,0:T(8,128)(2,1)S(1)}, bf16[512,768]{1,0:T(8,128)(2,1)S(1)}, u32[]{:S(2)}, u32[]{:S(2)}) collective-permute-start(bf16[512,768]{1,0:T(8,128)(2,1)S(1)} %get-tuple-element.22.have), channel_id=1, source_target_pairs={{0,1},{1,0},{2,3},{3,2},{4,5},{5,4},{6,7},{7,6},{8,9},{9,8},{10,11... | collective-permute-start | bytes 2359304 | tf_op jit(solution)/shard_map/ppermute | solution.py:234

commit v4 on v3

v4 whole, which is shorter than its diff:
```python
import jax
import jax.numpy as jnp
from jax import lax
from jax.experimental import pallas as pl
from jax.experimental.pallas import tpu as pltpu
from jax.sharding import PartitionSpec as P

BF = jnp.bfloat16
F32 = jnp.float32

Z_HI = [[4 * y + z for z in range(4)] for y in range(4)]
Y = [[4 * y + z for y in range(4)] for z in range(4)]
CHIPS = [[2 * chip + core for chip in range(16)] for core in range(2)]
PAIR = [(i, i ^ 1) for i in range(32)]
CHAIN = 0
VMEM = pl.BlockSpec(memory_space=pltpu.VMEM)
HBM = pl.BlockSpec(memory_space=pl.ANY)
LOOSE = pl.BlockSpec(memory_space=pltpu.VMEM)


def call(kernel, outs, *operands, specs=None, scratch=(), place=pltpu.VMEM, out_specs=None):
    specs = specs or [VMEM] * len(operands)
    operands = [
        pltpu.with_memory_space_constraint(a, pltpu.VMEM) if spec is VMEM else a
        for a, spec in zip(operands, specs)
    ]
    return pl.pallas_call(
        kernel,
        out_shape=tuple(place(shape, dtype) for shape, dtype in outs),
        in_specs=specs,
        out_specs=out_specs or (VMEM,) * len(outs),
        scratch_shapes=scratch,
        name=kernel.__name__,
    )(*operands)


def dot(a, b, over_a, over_b):
    return lax.dot_general(a, b, (((over_a,), (over_b,)), ((), ())), preferred_element_type=F32)


def spread(block, axis, groups):
    count = len(groups[0])
    copies = jnp.broadcast_to(block[None], (count,) + block.shape)
    return lax.all_to_all(copies, axis, 0, 0, tiled=True, axis_index_groups=groups)


UL, DR, RANKS, ALL = 3072, 3328, 3840, 3904


def pack_kernel(*refs):
    inputs, (down_right, up_left, lora_a, lora_b, send, ranks, sem) = refs[:6], refs[6:]
    copies = [(lora_a, ranks.at[0]), (lora_b, ranks.at[1])]
    copies += [(inputs[k], send.at[pl.ds(512 * k, 512)]) for k in range(6)]
    copies.append((up_left, send.at[pl.ds(UL, 256)]))
    copies.append((down_right, send.at[pl.ds(DR, 512)]))
    copies = [pltpu.make_async_copy(a, b, sem) for a, b in copies]
    for copy in copies:
        copy.start()
    for copy in copies:
        copy.wait()
    a, b = ranks[0].astype(F32), ranks[1].astype(F32)
    parts = [v[8 * m : 8 * m + 8] for m in range(4) for v in (a, b)]
    send[RANKS:ALL] = jnp.concatenate(parts, axis=0).astype(BF)


def pack(inputs, down_right, up_left, lora_a, lora_b):
    return call(
        pack_kernel,
        [((ALL, 128), BF)],
        *[a.reshape(512, 128) for a in inputs],
        down_right.reshape(512, 128),
        up_left.transpose(0, 2, 1).reshape(256, 128),
        lora_a.reshape(32, 128),
        lora_b.transpose(0, 2, 1).reshape(32, 128),
        specs=[HBM] * 10,
        scratch=[pltpu.VMEM((2, 32, 128), BF), pltpu.SemaphoreType.DMA],
    )[0]


def rows_of(own, other, k):
    at = slice(512 * k, 512 * k + 512)
    return jnp.concatenate([own[at], other[at]], axis=1)


def pick(rows, half, weight, over):
    low, high = [dot(rows(2 + 2 * half + i), weight, 1, over) for i in range(2)]
    return jnp.where(lax.broadcasted_iota(jnp.int32, low.shape, 1) < 64, low, high)


def first_kernel(own, other, part, ranks, far, sem):
    role = lax.rem(lax.axis_index("par") + CHAIN, 2)
    ranks[:64] = own[RANKS:ALL]
    ranks[64:] = other[RANKS:ALL]

    def put(at, value):
        part[:, :, at : at + value.shape[1]] = value.astype(BF).reshape(16, 32, value.shape[1])

    def right(m):
        at = slice(DR + 128 * m, DR + 128 * m + 128)
        return jnp.concatenate([own[at], other[at]], axis=0)

    @pl.when(role == 0)
    def _():
        hidden = rows_of(own, other, 0)
        put(0, dot(hidden, jnp.concatenate([right(0), right(1)], axis=1), 1, 0))
        put(256, dot(hidden, right(2), 1, 0))
        put(384, dot(rows_of(own, other, 1), right(3), 1, 0))
        left = jnp.concatenate([own[UL:DR], other[UL:DR]], axis=1)
        for half in range(2):
            weight = left[128 * half : 128 * half + 128]
            put(512 + 128 * half, pick(lambda k: rows_of(own, other, k), half, weight, 1))

    @pl.when(role == 1)
    def _():
        copy = pltpu.make_async_copy(other.at[pl.ds(0, UL)], far, sem)
        copy.start()
        copy.wait()


def first(own, other):
    shapes = [((16, 32, 768), BF), ((128, 128), BF), ((UL, 128), BF)]
    return call(
        first_kernel,
        shapes,
        own,
        other,
        scratch=[pltpu.SemaphoreType.DMA],
        place=jax.ShapeDtypeStruct,
        out_specs=(VMEM, VMEM, HBM),
    )


def parts_kernel(gathered, up_right, down_left, *refs):
    inputs, (far, keep, send) = refs[:6], refs[6:]
    nothing = jnp.zeros((16, 8, 128), F32)
    left_half = lax.broadcasted_iota(jnp.int32, (128, 128), 1) < 64
    side = [[], []]
    for m in range(4):
        pair = down_left[m // 2].astype(F32).T
        for_b = jnp.where(left_half if m % 2 == 0 else ~left_half, pair, 0.0)
        for_a = up_right[m].astype(F32)
        factor = jnp.concatenate(
            [
                jnp.concatenate([for_a.reshape(16, 8, 128), nothing], axis=1).reshape(256, 128),
                jnp.concatenate([nothing, for_b.reshape(16, 8, 128)], axis=1).reshape(256, 128),
            ],
            axis=1,
        ).astype(BF)
        for core in range(2):
            at = slice(64 * core + 16 * m, 64 * core + 16 * m + 16)
            ranks = gathered[:, at, :].reshape(256, 128)
            side[core].append(dot(ranks, factor, 0, 0).astype(BF))

    def weight(at, *modules):
        halves = [jnp.concatenate([half[m][:, at] for m in modules], axis=1) for half in side]
        return jnp.concatenate(halves, axis=0)

    def put(at, value):
        send[:, at : at + value.shape[1]] = value[:256].astype(BF)
        keep[:, at : at + value.shape[1]] = value[256:].astype(BF)

    x_at, g_at = slice(0, 128), slice(128, 256)
    def rows(k):
        return jnp.concatenate([inputs[k][...], far[512 * k : 512 * k + 512]], axis=1)

    hidden = rows(0)
    put(0, dot(hidden, weight(x_at, 0, 1), 1, 0))
    put(256, dot(hidden, weight(x_at, 2), 1, 0))
    put(384, dot(rows(1), weight(x_at, 3), 1, 0))
    for half in range(2):
        pair = weight(g_at, 2 * half) + weight(g_at, 2 * half + 1)
        put(512 + 128 * half, pick(rows, half, pair, 0))


def parts(gathered, up_right, down_left, inputs, other):
    return call(
        parts_kernel,
        [((256, 768), BF)] * 2,
        gathered,
        up_right,
        down_left,
        *inputs,
        other,
        specs=[VMEM, LOOSE, LOOSE] + [VMEM] * 7,
        place=jax.ShapeDtypeStruct,
    )


def join_kernel(keep, got, out):
    def add_up(full, parts):
        for e in range(2):
            at = slice(128 * e, 128 * e + 128)
            total = jnp.zeros((64, 128), F32)
            for m in range(4):
                x, g = slice(128 * m, 128 * m + 128), slice(512 + 64 * m, 576 + 64 * m)
                total += dot(full[at, g], parts[at, x], 0, 0)
                total += dot(parts[at, g], full[at, x], 0, 0)
            out[:, 2 * e : 2 * e + 2] = total.reshape(32, 2, 128)

    mover = lax.rem(lax.axis_index("par"), 2) == CHAIN

    @pl.when(mover)
    def _():
        add_up(keep, got)

    @pl.when(jnp.logical_not(mover))
    def _():
        add_up(got, keep)


def move_rows(part, ranks, up_right, down_left, inputs, other):
    pieces = lax.all_to_all(part, "par", 0, 0, tiled=True, axis_index_groups=CHIPS)
    total = jnp.sum(pieces.astype(F32), axis=0).astype(BF)
    full = spread(total, "par", CHIPS).reshape(2, 256, 768)
    return full[0], full[1]


def gather_ranks(part, ranks, up_right, down_left, inputs, other):
    along_z = spread(ranks, "ex", Z_HI).reshape(512, 128)
    gathered = spread(along_z, "ex", Y).reshape(16, 128, 128)
    return parts(gathered, up_right, down_left, inputs, other)


def per_device(*args):
    inputs, (lora_a, lora_b, up_left, up_right, down_left, down_right) = args[:6], args[6:]

    down_left = down_left.transpose(0, 2, 1).reshape(2, 128, 128)
    own = pack(inputs, down_right, up_left, lora_a, lora_b)
    other = lax.ppermute(own, "par", PAIR)
    part, ranks, far = first(own, other)
    mover = lax.axis_index("par") % 2 == CHAIN
    rows = [a.reshape(512, 128) for a in inputs]
    operands = part, ranks, up_right, down_left, rows, far
    keep, send = lax.cond(mover, move_rows, gather_ranks, *operands)
    got = lax.ppermute(send, "par", PAIR)
    out = call(join_kernel, [((32, 4, 128), F32)], keep, got)[0]
    out = lax.all_to_all(out, "par", 0, 0, tiled=True)
    out = jnp.sum(out.reshape(16, 4, 2, 128), axis=0) * (1.0 / 128)
    return out.reshape(4, 256)


def solution(mesh):
    in_specs = (P("ex", None, "par"),) * 6 + (
        P(None, "ex", "par"),
        P(None, "par", "ex"),
        P(None, "par", None),
        P(),
        P(),
        P(None, "par", None),
    )
    return jax.shard_map(
        per_device, mesh=mesh, in_specs=in_specs, out_specs=P("ex", "par"), check_vma=False
    )
```

time: 70 us -> 68.8 us (0.983)
  Pallas kernels: 4.42 us -> 3.61 us
    pallas_call x4, Pallas kernels: 4.42 us -> 3.61 us  [call(): pl.pallas_call(kernel, out_shape=tuple((place(shape, dtype) for shape, dt...]
where the time goes in v4:
time: 68.8 us; the launch traced here: 68.4 us
  blocking collectives  45.3 us (66%)
  starting transfers between devices  15.1 us (22%)
  Pallas kernels  3.61 us (5%)
  waiting for transfers between devices  3.44 us (5%)
  local copies, waits for them, and re-layouts  0.73 us (1%)
    all_to_all x2, blocking collectives, spread(): lax.all_to_all(copies, axis, 0, 0, tiled=True, axis_index_groups=groups)  34.1 us
    all_to_all x1, blocking collectives, per_device(): out = lax.all_to_all(out, 'par', 0, 0, tiled=True)  11.2 us
    ppermute x1, starting transfers between devices, per_device(): other = lax.ppermute(own, 'par', PAIR)  8.79 us
    ppermute x1, starting transfers between devices, per_device(): got = lax.ppermute(send, 'par', PAIR)  6.31 us
    pallas_call x4, Pallas kernels, call(): pl.pallas_call(kernel, out_shape=tuple((place(shape, dtype) for shape, dt...  3.61 us
    ppermute x1, waiting for transfers between devices, per_device(): other = lax.ppermute(own, 'par', PAIR)  2.11 us
  transfers between devices with their start and end apart: 2, of which 2 were waited for; matrix products, arithmetic and copies ran while one was open for 0% of the time, Pallas kernels for 0%

profile of v4, /device:TPU:1, one launch (start us, length us, event | category | flops | bytes accessed | tf_op | source)
XLA Modules:
  0.0 68.4 jit_solution(3614193227766609112)
XLA Ops:
  0.0 1.3 %pack_kernel.1.own = bf16[3904,128]{1,0:T(8,128)(2,1)S(1)} custom-call(bf16[512,128]{1,0:T(8,128)(2,1)} %bitcast.27, bf16[512,128]{1,0:T(8,128)(2,1)} %bitcast.29, bf16[512,128]{1,0:T(8,128)(2,1)} %bitcast.31, bf16[512,128]{1,0:T(8,128)(2,1)} %bitcast.33, bf16[512,128]{1,0:T(8,128)(2,1)} %bitcast.35, bf16[512,128]{1,0:T(8,128)(2,1)} %bitcast.37, ...), custom_call_target="tpu_custom_call" | custom-call | tf_op jit(solution)/shard_map/pack_kernel/pallas_call | solution.py:27
  1.3 8.8 %collective-permute-start = (bf16[3904,128]{1,0:T(8,128)(2,1)S(1)}, bf16[3904,128]{1,0:T(8,128)(2,1)S(1)}, u32[]{:S(2)}, u32[]{:S(2)}) collective-permute-start(bf16[3904,128]{1,0:T(8,128)(2,1)S(1)} %pack_kernel.1.own), channel_id=1, source_target_pairs={{0,1},{1,0},{2,3},{3,2},{4,5},{5,4},{6,7},{7,6},{8,9},{9,8},{10,11... | collective-permute-start | bytes 2998280 | tf_op jit(solution)/shard_map/ppermute | solution.py:229
  10.1 0.0 copy-start
  10.1 0.0 copy-start.1
  10.1 0.0 copy-start.2
  10.1 0.0 copy-start.3
  10.2 0.0 copy-start.4
  10.2 0.0 copy-start.7
  10.2 2.1 %collective-permute-done.other = bf16[3904,128]{1,0:T(8,128)(2,1)S(1)} collective-permute-done((bf16[3904,128]{1,0:T(8,128)(2,1)S(1)}, bf16[3904,128]{1,0:T(8,128)(2,1)S(1)}, u32[]{:S(2)}, u32[]{:S(2)}) %collective-permute-start) | collective-permute-done | bytes 999456 | tf_op jit(solution)/shard_map/ppermute | solution.py:229
  12.3 0.9 %first_kernel.1 = (bf16[16,32,768]{2,1,0:T(8,128)(2,1)}, bf16[128,128]{1,0:T(8,128)(2,1)S(1)}, bf16[3072,128]{1,0:T(8,128)(2,1)S(1)}) custom-call(bf16[3904,128]{1,0:T(8,128)(2,1)S(1)} %pack_kernel.1.own, bf16[3904,128]{1,0:T(8,128)(2,1)S(1)} %collective-permute-done.other), custom_call_target="tpu_custom_call" | custom-call | tf_op jit(solution)/shard_map/first_kernel/pallas_call | solution.py:27
  13.2 0.0 copy-done
  13.3 0.0 copy-done.1
  13.3 0.0 copy-done.2
  13.3 0.0 copy-done.3
  13.3 0.0 copy-done.4
  13.3 0.0 copy-done.7
  13.3 35.3 %conditional.1 = ((bf16[256,768]{1,0:T(8,128)(2,1)S(1)}, bf16[256,768]{1,0:T(8,128)(2,1)S(1)})) conditional(s32[]{:T(128)} %convert_element_type.2, (bf16[128,128]{1,0:T(8,128)(2,1)S(1)}, bf16[4,64,128]{2,1,0:T(8,128)(2,1)S(1)}, bf16[4,128,128]{2,1,0:T(8,128)(2,1)}, bf16[512,128]{1,0:T(8,128)(2,1)S(1)}, bf16[512,128]{1,0:T(8,128)(2,1)S(1)}, ...), branch_computations={%region_0.1_spmd, %region_1.3_spmd} | conditional | flops 368640 | bytes 6389786 | solution.py:234
  13.3 23.1 %all_to_all.21 = bf16[4,128,128]{2,1,0:T(8,128)(2,1)S(1)} all-to-all(bf16[4,128,128]{2,1,0:T(8,128)(2,1)S(1)} %broadcast_in_dim.1), channel_id=1, replica_groups={{0,32,64,96},{128,160,192,224},{256,288,320,352},{384,416,448,480},{1,3..., dimensions={0} | all-to-all | bytes 262144 | tf_op jit(solution)/shard_map/cond/branch_0_fun/all_to_all | solution.py:44
  36.4 0.1 broadcast_in_dim.6
  36.5 0.0 copy-start.5
  36.5 0.0 copy-start.6
  36.5 11.1 %all_to_all.22 = bf16[4,512,128]{2,1,0:T(8,128)(2,1)S(1)} all-to-all(bf16[4,512,128]{2,1,0:T(8,128)(2,1)S(1)} %broadcast_in_dim.6), channel_id=1, replica_groups={{0,128,256,384},{32,160,288,416},{64,192,320,448},{96,224,352,480},{1,1..., dimensions={0} | all-to-all | bytes 1048576 | tf_op jit(solution)/shard_map/cond/branch_0_fun/all_to_all | solution.py:44
  47.6 0.0 copy-done.5
  47.6 0.0 copy-done.6
  47.6 1.0 %parts_kernel.1 = (bf16[256,768]{1,0:T(8,128)(2,1)S(1)}, bf16[256,768]{1,0:T(8,128)(2,1)S(1)}) custom-call(bf16[16,128,128]{2,1,0:T(8,128)(2,1)S(1)} %bitcast.26, bf16[4,128,128]{2,1,0:T(8,128)(2,1)S(1)} %copy-done.6, bf16[2,128,128]{2,1,0:T(8,128)(2,1)S(1)} %bitcast.45, bf16[512,128]{1,0:T(8,128)(2,1)S(1)} %get-tuple-element.30.refs_0_, ...), custom_call_target="tpu_custom_call" | custom-call | tf_op jit(solution)/shard_map/cond/branch_0_fun/parts_kernel/pallas_call | solution.py:27
  48.6 6.3 %collective-permute-start.1 = (bf16[256,768]{1,0:T(8,128)(2,1)S(1)}, bf16[256,768]{1,0:T(8,128)(2,1)S(1)}, u32[]{:S(2)}, u32[]{:S(2)}) collective-permute-start(bf16[256,768]{1,0:T(8,128)(2,1)S(1)} %get-tuple-element.46), channel_id=1, source_target_pairs={{0,1},{1,0},{2,3},{3,2},{4,5},{5,4},{6,7},{7,6},{8,9},{9,8},{10,11... | collective-permute-start | bytes 1179656 | tf_op jit(solution)/shard_map/ppermute | solution.py:235
  54.9 1.3 %collective-permute-done.1.got = bf16[256,768]{1,0:T(8,128)(2,1)S(1)} collective-permute-done((bf16[256,768]{1,0:T(8,128)(2,1)S(1)}, bf16[256,768]{1,0:T(8,128)(2,1)S(1)}, u32[]{:S(2)}, u32[]{:S(2)}) %collective-permute-start.1) | collective-permute-done | bytes 393248 | tf_op jit(solution)/shard_map/ppermute | solution.py:235
  56.2 0.4 join_kernel.1
  56.6 11.2 %all_to_all.25 = f32[32,4,128]{2,1,0:T(4,128)S(1)} all-to-all(f32[32,4,128]{2,1,0:T(4,128)S(1)} %join_kernel.1), channel_id=1, replica_groups=mesh['ex'=16,'par'=32] {'par'}, dimensions={0} | all-to-all | bytes 131072 | tf_op jit(solution)/shard_map/all_to_all | solution.py:237
  67.8 0.6 copy.16
  (3 shorter events, 0.1 us)
Async XLA Ops:
  1.3 11.0 %collective-permute-start = (bf16[3904,128]{1,0:T(8,128)(2,1)S(1)}, bf16[3904,128]{1,0:T(8,128)(2,1)S(1)}, u32[]{:S(2)}, u32[]{:S(2)}) collective-permute-start(bf16[3904,128]{1,0:T(8,128)(2,1)S(1)} %pack_kernel.1.own), channel_id=1, source_target_pairs={{0,1},{1,0},{2,3},{3,2},{4,5},{5,4},{6,7},{7,6},{8,9},{9,8},{10,11... | collective-permute-start | bytes 2998280 | tf_op jit(solution)/shard_map/ppermute | solution.py:229
  10.1 3.1 %copy-start = (bf16[4,128,128]{2,1,0:T(8,128)(2,1)S(1)}, bf16[4,128,128]{2,1,0:T(8,128)(2,1)}, u32[]{:S(2)}) copy-start(bf16[4,128,128]{2,1,0:T(8,128)(2,1)} %param.14) | copy-start | bytes 393220
  10.1 3.1 %copy-start.1 = (bf16[4,128,128]{2,1,0:T(8,128)(2,1)S(1)}, bf16[4,128,128]{2,1,0:T(8,128)(2,1)}, u32[]{:S(2)}) copy-start(bf16[4,128,128]{2,1,0:T(8,128)(2,1)} %param.15) | copy-start | bytes 393220
  10.1 3.1 %copy-start.2 = (bf16[4,128,128]{2,1,0:T(8,128)(2,1)S(1)}, bf16[4,128,128]{2,1,0:T(8,128)(2,1)}, u32[]{:S(2)}) copy-start(bf16[4,128,128]{2,1,0:T(8,128)(2,1)} %param.16) | copy-start | bytes 393220
  10.1 3.1 %copy-start.3 = (bf16[4,128,128]{2,1,0:T(8,128)(2,1)S(1)}, bf16[4,128,128]{2,1,0:T(8,128)(2,1)}, u32[]{:S(2)}) copy-start(bf16[4,128,128]{2,1,0:T(8,128)(2,1)} %param.17) | copy-start | bytes 393220
  10.2 3.1 %copy-start.4 = (bf16[4,128,128]{2,1,0:T(8,128)(2,1)S(1)}, bf16[4,128,128]{2,1,0:T(8,128)(2,1)}, u32[]{:S(2)}) copy-start(bf16[4,128,128]{2,1,0:T(8,128)(2,1)} %param.18) | copy-start | bytes 393220
  10.2 3.1 %copy-start.7 = (bf16[4,128,64]{1,2,0:T(8,128)(2,1)S(1)}, bf16[4,128,64]{1,2,0:T(8,128)(2,1)}, u32[]{:S(2)}) copy-start(bf16[4,128,64]{1,2,0:T(8,128)(2,1)} %param.24) | copy-start | bytes 196612
  36.5 11.1 %copy-start.5 = (bf16[512,128]{1,0:T(8,128)(2,1)S(1)}, bf16[512,128]{1,0:T(8,128)(2,1)}, u32[]{:S(2)}) copy-start(bf16[512,128]{1,0:T(8,128)(2,1)} %get-tuple-element.35.refs_5_) | copy-start | bytes 393220 | tf_op jit(solution)/shard_map/cond
  36.5 11.1 %copy-start.6 = (bf16[4,128,128]{2,1,0:T(8,128)(2,1)S(1)}, bf16[4,128,128]{2,1,0:T(8,128)(2,1)}, u32[]{:S(2)}) copy-start(bf16[4,128,128]{2,1,0:T(8,128)(2,1)} %get-tuple-element.48.up_right) | copy-start | bytes 393220 | tf_op jit(solution)/shard_map/cond
  48.6 7.6 %collective-permute-start.1 = (bf16[256,768]{1,0:T(8,128)(2,1)S(1)}, bf16[256,768]{1,0:T(8,128)(2,1)S(1)}, u32[]{:S(2)}, u32[]{:S(2)}) collective-permute-start(bf16[256,768]{1,0:T(8,128)(2,1)S(1)} %get-tuple-element.46), channel_id=1, source_target_pairs={{0,1},{1,0},{2,3},{3,2},{4,5},{5,4},{6,7},{7,6},{8,9},{9,8},{10,11... | collective-permute-start | bytes 1179656 | tf_op jit(solution)/shard_map/ppermute | solution.py:235

commit v5 on v4

--- a/solution.py
+++ b/solution.py
@@ -12,7 +12,7 @@
 Y = [[4 * y + z for y in range(4)] for z in range(4)]
 CHIPS = [[2 * chip + core for chip in range(16)] for core in range(2)]
 PAIR = [(i, i ^ 1) for i in range(32)]
-CHAIN = 0
+CHAIN = 1
 VMEM = pl.BlockSpec(memory_space=pltpu.VMEM)
 HBM = pl.BlockSpec(memory_space=pl.ANY)
 LOOSE = pl.BlockSpec(memory_space=pltpu.VMEM)
@@ -130,22 +130,27 @@
     )
 
 
+ORDER = (0, 1, 3, 2)
+
+
 def parts_kernel(gathered, up_right, down_left, *refs):
-    inputs, (far, keep, send) = refs[:6], refs[6:]
-    nothing = jnp.zeros((16, 8, 128), F32)
-    left_half = lax.broadcasted_iota(jnp.int32, (128, 128), 1) < 64
+    inputs, (far, keep, send, for_a, for_b) = refs[:6], refs[6:]
+    for m in range(4):
+        for_a[m] = up_right[m].astype(F32)
+    for half in range(2):
+        for_b[half] = down_left[half].astype(F32).T
+    z_hi = jnp.bitwise_and(lax.axis_index("ex"), 3)
+    owners = [4 * y + jnp.bitwise_xor(z_hi, k) for y in range(4) for k in ORDER]
+    owners = [pl.ds(pl.multiple_of(8 * owner, 8), 8) for owner in owners]
+    nothing = jnp.zeros((8, 128), F32)
+    left_half = lax.broadcasted_iota(jnp.int32, (256, 128), 1) < 64
     side = [[], []]
     for m in range(4):
-        pair = down_left[m // 2].astype(F32).T
-        for_b = jnp.where(left_half if m % 2 == 0 else ~left_half, pair, 0.0)
-        for_a = up_right[m].astype(F32)
-        factor = jnp.concatenate(
-            [
-                jnp.concatenate([for_a.reshape(16, 8, 128), nothing], axis=1).reshape(256, 128),
-                jnp.concatenate([nothing, for_b.reshape(16, 8, 128)], axis=1).reshape(256, 128),
-            ],
-            axis=1,
-        ).astype(BF)
+        rows_a = [part for at in owners for part in (for_a[m, at, :], nothing)]
+        rows_b = [part for at in owners for part in (nothing, for_b[m // 2, at, :])]
+        rows_b = jnp.concatenate(rows_b, axis=0)
+        rows_b = jnp.where(left_half if m % 2 == 0 else ~left_half, rows_b, 0.0)
+        factor = jnp.concatenate([jnp.concatenate(rows_a, axis=0), rows_b], axis=1).astype(BF)
         for core in range(2):
             at = slice(64 * core + 16 * m, 64 * core + 16 * m + 16)
             ranks = gathered[:, at, :].reshape(256, 128)
@@ -182,6 +187,7 @@
         *inputs,
         other,
         specs=[VMEM, LOOSE, LOOSE] + [VMEM] * 7,
+        scratch=[pltpu.VMEM((4, 128, 128), F32), pltpu.VMEM((2, 128, 128), F32)],
         place=jax.ShapeDtypeStruct,
     )
 
@@ -215,8 +221,14 @@
     return full[0], full[1]
 
 
+def swap(block, step):
+    places = [(32 * e + p, 32 * (e ^ step) + p) for e in range(16) for p in range(1 - CHAIN, 32, 2)]
+    return lax.ppermute(block, ("ex", "par"), places)
+
+
 def gather_ranks(part, ranks, up_right, down_left, inputs, other):
-    along_z = spread(ranks, "ex", Z_HI).reshape(512, 128)
+    two = jnp.stack([ranks, swap(ranks, 1)])
+    along_z = jnp.concatenate([two, swap(two, 3)]).reshape(512, 128)
     gathered = spread(along_z, "ex", Y).reshape(16, 128, 128)
     return parts(gathered, up_right, down_left, inputs, other)
 
@@ -236,6 +248,7 @@
     out = call(join_kernel, [((32, 4, 128), F32)], keep, got)[0]
     out = lax.all_to_all(out, "par", 0, 0, tiled=True)
     out = jnp.sum(out.reshape(16, 4, 2, 128), axis=0) * (1.0 / 128)
+    out = jnp.concatenate([out[2:], out[:2]])
     return out.reshape(4, 256)
 
 

time: 68.8 us -> 67 us (0.974)
  starting transfers between devices: 15.1 us -> 10.7 us
  blocking collectives: 45.3 us -> 47.8 us
    all_to_all x0 -> x1, blocking collectives: none -> 17.5 us  [move_rows(): lax.all_to_all(part, 'par', 0, 0, tiled=True, axis_index_groups=CHIPS)]
    all_to_all x2 -> x1, blocking collectives: 34.1 us -> 17.1 us  [spread(): lax.all_to_all(copies, axis, 0, 0, tiled=True, axis_index_groups=groups)]
    ppermute x1, starting transfers between devices: 6.31 us -> 1.92 us  [per_device(): got = lax.ppermute(send, 'par', PAIR)]
    all_to_all x1, blocking collectives: 11.2 us -> 13.2 us  [per_device(): out = lax.all_to_all(out, 'par', 0, 0, tiled=True)]
    pallas_call x4 -> x3, Pallas kernels: 3.61 us -> 3.25 us  [call(): pl.pallas_call(kernel, out_shape=tuple((place(shape, dtype) for shape, dt...]
where the time goes in v5:
time: 67 us; the launch traced here: 66.6 us
  blocking collectives  47.8 us (71%)
  starting transfers between devices  10.7 us (16%)
  waiting for transfers between devices  3.8 us (6%)
  Pallas kernels  3.25 us (5%)
  local copies, waits for them, and re-layouts  0.76 us (1%)
    all_to_all x1, blocking collectives, move_rows(): lax.all_to_all(part, 'par', 0, 0, tiled=True, axis_index_groups=CHIPS)  17.5 us
    all_to_all x1, blocking collectives, spread(): lax.all_to_all(copies, axis, 0, 0, tiled=True, axis_index_groups=groups)  17.1 us
    all_to_all x1, blocking collectives, per_device(): out = lax.all_to_all(out, 'par', 0, 0, tiled=True)  13.2 us
    ppermute x1, starting transfers between devices, per_device(): other = lax.ppermute(own, 'par', PAIR)  8.79 us
    pallas_call x3, Pallas kernels, call(): pl.pallas_call(kernel, out_shape=tuple((place(shape, dtype) for shape, dt...  3.25 us
    ppermute x1, waiting for transfers between devices, per_device(): other = lax.ppermute(own, 'par', PAIR)  2.11 us
    ppermute x1, starting transfers between devices, per_device(): got = lax.ppermute(send, 'par', PAIR)  1.92 us
    ppermute x1, waiting for transfers between devices, per_device(): got = lax.ppermute(send, 'par', PAIR)  1.69 us
  transfers between devices with their start and end apart: 2, of which 2 were waited for; matrix products, arithmetic and copies ran while one was open for 0% of the time, Pallas kernels for 0%

profile of v5, /device:TPU:1, one launch (start us, length us, event | category | flops | bytes accessed | tf_op | source)
XLA Modules:
  0.0 66.6 jit_solution(18195727337242567547)
XLA Ops:
  0.0 1.3 %pack_kernel.1.own = bf16[3904,128]{1,0:T(8,128)(2,1)S(1)} custom-call(bf16[512,128]{1,0:T(8,128)(2,1)} %bitcast.29, bf16[512,128]{1,0:T(8,128)(2,1)} %bitcast.31, bf16[512,128]{1,0:T(8,128)(2,1)} %bitcast.33, bf16[512,128]{1,0:T(8,128)(2,1)} %bitcast.35, bf16[512,128]{1,0:T(8,128)(2,1)} %bitcast.37, bf16[512,128]{1,0:T(8,128)(2,1)} %bitcast.39, ...), custom_call_target="tpu_custom_call" | custom-call | tf_op jit(solution)/shard_map/pack_kernel/pallas_call | solution.py:27
  1.3 8.8 %collective-permute-start.2 = (bf16[3904,128]{1,0:T(8,128)(2,1)S(1)}, bf16[3904,128]{1,0:T(8,128)(2,1)S(1)}, u32[]{:S(2)}, u32[]{:S(2)}) collective-permute-start(bf16[3904,128]{1,0:T(8,128)(2,1)S(1)} %pack_kernel.1.own), channel_id=1, source_target_pairs={{0,1},{1,0},{2,3},{3,2},{4,5},{5,4},{6,7},{7,6},{8,9},{9,8},{10,11... | collective-permute-start | bytes 2998280 | tf_op jit(solution)/shard_map/ppermute | solution.py:241
  10.1 0.0 copy-start
  10.1 0.0 copy-start.1
  10.1 0.0 copy-start.2
  10.1 0.0 copy-start.3
  10.2 0.0 copy-start.4
  10.2 0.0 copy-start.7
  10.2 2.1 %collective-permute-done.2.other = bf16[3904,128]{1,0:T(8,128)(2,1)S(1)} collective-permute-done((bf16[3904,128]{1,0:T(8,128)(2,1)S(1)}, bf16[3904,128]{1,0:T(8,128)(2,1)S(1)}, u32[]{:S(2)}, u32[]{:S(2)}) %collective-permute-start.2) | collective-permute-done | bytes 999456 | tf_op jit(solution)/shard_map/ppermute | solution.py:241
  12.3 1.5 %first_kernel.1 = (bf16[16,32,768]{2,1,0:T(8,128)(2,1)}, bf16[128,128]{1,0:T(8,128)(2,1)S(1)}, bf16[3072,128]{1,0:T(8,128)(2,1)S(1)}) custom-call(bf16[3904,128]{1,0:T(8,128)(2,1)S(1)} %pack_kernel.1.own, bf16[3904,128]{1,0:T(8,128)(2,1)S(1)} %collective-permute-done.2.other), custom_call_target="tpu_custom_call" | custom-call | tf_op jit(solution)/shard_map/first_kernel/pallas_call | solution.py:27
  13.8 0.0 copy-done
  13.9 0.0 copy-done.1
  13.9 0.0 copy-done.2
  13.9 0.0 copy-done.3
  13.9 0.0 copy-done.4
  13.9 0.0 copy-done.7
  13.9 34.9 %conditional.1 = ((bf16[256,768]{1,0:T(8,128)(2,1)S(1)}, bf16[256,768]{1,0:T(8,128)(2,1)S(1)})) conditional(s32[]{:T(128)} %convert_element_type.2, (bf16[128,128]{1,0:T(8,128)(2,1)S(1)}, bf16[4,64,128]{2,1,0:T(8,128)(2,1)S(1)}, bf16[4,128,128]{2,1,0:T(8,128)(2,1)}, bf16[512,128]{1,0:T(8,128)(2,1)S(1)}, bf16[512,128]{1,0:T(8,128)(2,1)S(1)}, ...), branch_computations={%region_0.1_spmd, %region_1.3_spmd} | conditional | flops 368640 | bytes 6389786 | solution.py:246
  13.9 17.5 %all_to_all.18 = bf16[16,32,768]{2,1,0:T(8,128)(2,1)S(1)} all-to-all(bf16[16,32,768]{2,1,0:T(8,128)(2,1)} %param.1), channel_id=1, replica_groups={{0,2,4,6,8,10,12,14,16,18,20,22,24,26,28,30},{1,3,5,7,9,11,13,15,17,19,..., dimensions={0} | all-to-all | bytes 1572864 | tf_op jit(solution)/shard_map/cond/branch_1_fun/all_to_all | solution.py:218
  31.5 0.1 reduce_sum.19
  31.6 0.1 broadcast_in_dim.8
  31.7 17.1 %all_to_all.19 = bf16[16,32,768]{2,1,0:T(8,128)(2,1)S(1)} all-to-all(bf16[16,32,768]{2,1,0:T(8,128)(2,1)S(1)} %broadcast_in_dim.8), channel_id=1, replica_groups={{0,2,4,6,8,10,12,14,16,18,20,22,24,26,28,30},{1,3,5,7,9,11,13,15,17,19,..., dimensions={0} | all-to-all | bytes 1572864 | tf_op jit(solution)/shard_map/cond/branch_1_fun/all_to_all | solution.py:44
  48.7 0.1 fusion
  48.8 1.9 %collective-permute-start.3 = (bf16[256,768]{1,0:T(8,128)(2,1)S(1)}, bf16[256,768]{1,0:T(8,128)(2,1)S(1)}, u32[]{:S(2)}, u32[]{:S(2)}) collective-permute-start(bf16[256,768]{1,0:T(8,128)(2,1)S(1)} %get-tuple-element.46), channel_id=1, source_target_pairs={{0,1},{1,0},{2,3},{3,2},{4,5},{5,4},{6,7},{7,6},{8,9},{9,8},{10,11... | collective-permute-start | bytes 1179656 | tf_op jit(solution)/shard_map/ppermute | solution.py:247
  50.7 1.7 %collective-permute-done.3.got = bf16[256,768]{1,0:T(8,128)(2,1)S(1)} collective-permute-done((bf16[256,768]{1,0:T(8,128)(2,1)S(1)}, bf16[256,768]{1,0:T(8,128)(2,1)S(1)}, u32[]{:S(2)}, u32[]{:S(2)}) %collective-permute-start.3) | collective-permute-done | bytes 393248 | tf_op jit(solution)/shard_map/ppermute | solution.py:247
  52.4 0.4 join_kernel.1
  52.8 13.2 %all_to_all.20 = f32[32,4,128]{2,1,0:T(4,128)S(1)} all-to-all(f32[32,4,128]{2,1,0:T(4,128)S(1)} %join_kernel.1), channel_id=1, replica_groups=mesh['ex'=16,'par'=32] {'par'}, dimensions={0} | all-to-all | bytes 131072 | tf_op jit(solution)/shard_map/all_to_all | solution.py:249
  66.1 0.6 copy.16
  (4 shorter events, 0.1 us)
Async XLA Ops:
  1.3 11.0 %collective-permute-start.2 = (bf16[3904,128]{1,0:T(8,128)(2,1)S(1)}, bf16[3904,128]{1,0:T(8,128)(2,1)S(1)}, u32[]{:S(2)}, u32[]{:S(2)}) collective-permute-start(bf16[3904,128]{1,0:T(8,128)(2,1)S(1)} %pack_kernel.1.own), channel_id=1, source_target_pairs={{0,1},{1,0},{2,3},{3,2},{4,5},{5,4},{6,7},{7,6},{8,9},{9,8},{10,11... | collective-permute-start | bytes 2998280 | tf_op jit(solution)/shard_map/ppermute | solution.py:241
  10.1 3.7 %copy-start = (bf16[4,128,128]{2,1,0:T(8,128)(2,1)S(1)}, bf16[4,128,128]{2,1,0:T(8,128)(2,1)}, u32[]{:S(2)}) copy-start(bf16[4,128,128]{2,1,0:T(8,128)(2,1)} %param.14) | copy-start | bytes 393220
  10.1 3.7 %copy-start.1 = (bf16[4,128,128]{2,1,0:T(8,128)(2,1)S(1)}, bf16[4,128,128]{2,1,0:T(8,128)(2,1)}, u32[]{:S(2)}) copy-start(bf16[4,128,128]{2,1,0:T(8,128)(2,1)} %param.15) | copy-start | bytes 393220
  10.1 3.7 %copy-start.2 = (bf16[4,128,128]{2,1,0:T(8,128)(2,1)S(1)}, bf16[4,128,128]{2,1,0:T(8,128)(2,1)}, u32[]{:S(2)}) copy-start(bf16[4,128,128]{2,1,0:T(8,128)(2,1)} %param.16) | copy-start | bytes 393220
  10.1 3.7 %copy-start.3 = (bf16[4,128,128]{2,1,0:T(8,128)(2,1)S(1)}, bf16[4,128,128]{2,1,0:T(8,128)(2,1)}, u32[]{:S(2)}) copy-start(bf16[4,128,128]{2,1,0:T(8,128)(2,1)} %param.17) | copy-start | bytes 393220
  10.2 3.7 %copy-start.4 = (bf16[4,128,128]{2,1,0:T(8,128)(2,1)S(1)}, bf16[4,128,128]{2,1,0:T(8,128)(2,1)}, u32[]{:S(2)}) copy-start(bf16[4,128,128]{2,1,0:T(8,128)(2,1)} %param.18) | copy-start | bytes 393220
  10.2 3.7 %copy-start.7 = (bf16[4,128,64]{1,2,0:T(8,128)(2,1)S(1)}, bf16[4,128,64]{1,2,0:T(8,128)(2,1)}, u32[]{:S(2)}) copy-start(bf16[4,128,64]{1,2,0:T(8,128)(2,1)} %param.24) | copy-start | bytes 196612
  48.8 3.6 %collective-permute-start.3 = (bf16[256,768]{1,0:T(8,128)(2,1)S(1)}, bf16[256,768]{1,0:T(8,128)(2,1)S(1)}, u32[]{:S(2)}, u32[]{:S(2)}) collective-permute-start(bf16[256,768]{1,0:T(8,128)(2,1)S(1)} %get-tuple-element.46), channel_id=1, source_target_pairs={{0,1},{1,0},{2,3},{3,2},{4,5},{5,4},{6,7},{7,6},{8,9},{9,8},{10,11... | collective-permute-start | bytes 1179656 | tf_op jit(solution)/shard_map/ppermute | solution.py:247

commit v6 on v5

--- a/solution.py
+++ b/solution.py
@@ -87,13 +87,17 @@
     return jnp.where(lax.broadcasted_iota(jnp.int32, low.shape, 1) < 64, low, high)
 
 
-def first_kernel(own, other, part, ranks, far, sem):
+def first_kernel(own, other, part, ranks, far, rows, sem):
     role = lax.rem(lax.axis_index("par") + CHAIN, 2)
     ranks[:64] = own[RANKS:ALL]
     ranks[64:] = other[RANKS:ALL]
+    copies = []
 
     def put(at, value):
-        part[:, :, at : at + value.shape[1]] = value.astype(BF).reshape(16, 32, value.shape[1])
+        columns = slice(at, at + value.shape[1])
+        rows[:, :, columns] = value.astype(BF).reshape(16, 32, value.shape[1])
+        copies.append(pltpu.make_async_copy(rows.at[:, :, columns], part.at[:, :, columns], sem))
+        copies[-1].start()
 
     def right(m):
         at = slice(DR + 128 * m, DR + 128 * m + 128)
@@ -101,14 +105,16 @@
 
     @pl.when(role == 0)
     def _():
+        left = jnp.concatenate([own[UL:DR], other[UL:DR]], axis=1)
+        for half in range(2):
+            weight = left[128 * half : 128 * half + 128]
+            put(512 + 128 * half, pick(lambda k: rows_of(own, other, k), half, weight, 1))
         hidden = rows_of(own, other, 0)
         put(0, dot(hidden, jnp.concatenate([right(0), right(1)], axis=1), 1, 0))
         put(256, dot(hidden, right(2), 1, 0))
         put(384, dot(rows_of(own, other, 1), right(3), 1, 0))
-        left = jnp.concatenate([own[UL:DR], other[UL:DR]], axis=1)
-        for half in range(2):
-            weight = left[128 * half : 128 * half + 128]
-            put(512 + 128 * half, pick(lambda k: rows_of(own, other, k), half, weight, 1))
+        for copy in copies:
+            copy.wait()
 
     @pl.when(role == 1)
     def _():
@@ -124,9 +130,9 @@
         shapes,
         own,
         other,
-        scratch=[pltpu.SemaphoreType.DMA],
+        scratch=[pltpu.VMEM((16, 32, 768), BF), pltpu.SemaphoreType.DMA],
         place=jax.ShapeDtypeStruct,
-        out_specs=(VMEM, VMEM, HBM),
+        out_specs=(HBM, VMEM, HBM),
     )
 
 

time: 67 us -> 66.2 us (0.988)
  no operation moved by 1% of the time
where the time goes in v6:
time: 66.2 us; the launch traced here: 65.9 us
  blocking collectives  47.2 us (71%)
  starting transfers between devices  10.7 us (16%)
  waiting for transfers between devices  3.8 us (6%)
  Pallas kernels  3.12 us (5%)
  local copies, waits for them, and re-layouts  0.76 us (1%)
    all_to_all x1, blocking collectives, move_rows(): lax.all_to_all(part, 'par', 0, 0, tiled=True, axis_index_groups=CHIPS)  17.5 us
    all_to_all x1, blocking collectives, spread(): lax.all_to_all(copies, axis, 0, 0, tiled=True, axis_index_groups=groups)  16.6 us
    all_to_all x1, blocking collectives, per_device(): out = lax.all_to_all(out, 'par', 0, 0, tiled=True)  13 us
    ppermute x1, starting transfers between devices, per_device(): other = lax.ppermute(own, 'par', PAIR)  8.79 us
    pallas_call x3, Pallas kernels, call(): pl.pallas_call(kernel, out_shape=tuple((place(shape, dtype) for shape, dt...  3.12 us
    ppermute x1, waiting for transfers between devices, per_device(): other = lax.ppermute(own, 'par', PAIR)  2.11 us
    ppermute x1, starting transfers between devices, per_device(): got = lax.ppermute(send, 'par', PAIR)  1.92 us
    ppermute x1, waiting for transfers between devices, per_device(): got = lax.ppermute(send, 'par', PAIR)  1.69 us
  transfers between devices with their start and end apart: 2, of which 2 were waited for; matrix products, arithmetic and copies ran while one was open for 0% of the time, Pallas kernels for 0%

profile of v6, /device:TPU:1, one launch (start us, length us, event | category | flops | bytes accessed | tf_op | source)
XLA Modules:
  0.0 65.9 jit_solution(18331583019975472716)
XLA Ops:
  0.0 1.3 %pack_kernel.1.own = bf16[3904,128]{1,0:T(8,128)(2,1)S(1)} custom-call(bf16[512,128]{1,0:T(8,128)(2,1)} %bitcast.29, bf16[512,128]{1,0:T(8,128)(2,1)} %bitcast.31, bf16[512,128]{1,0:T(8,128)(2,1)} %bitcast.33, bf16[512,128]{1,0:T(8,128)(2,1)} %bitcast.35, bf16[512,128]{1,0:T(8,128)(2,1)} %bitcast.37, bf16[512,128]{1,0:T(8,128)(2,1)} %bitcast.39, ...), custom_call_target="tpu_custom_call" | custom-call | tf_op jit(solution)/shard_map/pack_kernel/pallas_call | solution.py:27
  1.3 8.8 %collective-permute-start.2 = (bf16[3904,128]{1,0:T(8,128)(2,1)S(1)}, bf16[3904,128]{1,0:T(8,128)(2,1)S(1)}, u32[]{:S(2)}, u32[]{:S(2)}) collective-permute-start(bf16[3904,128]{1,0:T(8,128)(2,1)S(1)} %pack_kernel.1.own), channel_id=1, source_target_pairs={{0,1},{1,0},{2,3},{3,2},{4,5},{5,4},{6,7},{7,6},{8,9},{9,8},{10,11... | collective-permute-start | bytes 2998280 | tf_op jit(solution)/shard_map/ppermute | solution.py:247
  10.1 0.0 copy-start
  10.1 0.0 copy-start.1
  10.1 0.0 copy-start.2
  10.1 0.0 copy-start.3
  10.2 0.0 copy-start.4
  10.2 0.0 copy-start.7
  10.2 2.1 %collective-permute-done.2.other = bf16[3904,128]{1,0:T(8,128)(2,1)S(1)} collective-permute-done((bf16[3904,128]{1,0:T(8,128)(2,1)S(1)}, bf16[3904,128]{1,0:T(8,128)(2,1)S(1)}, u32[]{:S(2)}, u32[]{:S(2)}) %collective-permute-start.2) | collective-permute-done | bytes 999456 | tf_op jit(solution)/shard_map/ppermute | solution.py:247
  12.3 1.4 %first_kernel.1 = (bf16[16,32,768]{2,1,0:T(8,128)(2,1)}, bf16[128,128]{1,0:T(8,128)(2,1)S(1)}, bf16[3072,128]{1,0:T(8,128)(2,1)S(1)}) custom-call(bf16[3904,128]{1,0:T(8,128)(2,1)S(1)} %pack_kernel.1.own, bf16[3904,128]{1,0:T(8,128)(2,1)S(1)} %collective-permute-done.2.other), custom_call_target="tpu_custom_call" | custom-call | tf_op jit(solution)/shard_map/first_kernel/pallas_call | solution.py:27
  13.7 0.0 copy-done
  13.7 0.0 copy-done.1
  13.7 0.0 copy-done.2
  13.7 0.0 copy-done.3
  13.7 0.0 copy-done.4
  13.8 0.0 copy-done.7
  13.8 34.4 %conditional.1 = ((bf16[256,768]{1,0:T(8,128)(2,1)S(1)}, bf16[256,768]{1,0:T(8,128)(2,1)S(1)})) conditional(s32[]{:T(128)} %convert_element_type.2, (bf16[128,128]{1,0:T(8,128)(2,1)S(1)}, bf16[4,64,128]{2,1,0:T(8,128)(2,1)S(1)}, bf16[4,128,128]{2,1,0:T(8,128)(2,1)}, bf16[512,128]{1,0:T(8,128)(2,1)S(1)}, bf16[512,128]{1,0:T(8,128)(2,1)S(1)}, ...), branch_computations={%region_0.1_spmd, %region_1.3_spmd} | conditional | flops 368640 | bytes 6389786 | solution.py:252
  13.8 17.5 %all_to_all.18 = bf16[16,32,768]{2,1,0:T(8,128)(2,1)S(1)} all-to-all(bf16[16,32,768]{2,1,0:T(8,128)(2,1)} %param.1), channel_id=1, replica_groups={{0,2,4,6,8,10,12,14,16,18,20,22,24,26,28,30},{1,3,5,7,9,11,13,15,17,19,..., dimensions={0} | all-to-all | bytes 1572864 | tf_op jit(solution)/shard_map/cond/branch_1_fun/all_to_all | solution.py:224
  31.3 0.1 reduce_sum.19
  31.4 0.1 broadcast_in_dim.8
  31.5 16.6 %all_to_all.19 = bf16[16,32,768]{2,1,0:T(8,128)(2,1)S(1)} all-to-all(bf16[16,32,768]{2,1,0:T(8,128)(2,1)S(1)} %broadcast_in_dim.8), channel_id=1, replica_groups={{0,2,4,6,8,10,12,14,16,18,20,22,24,26,28,30},{1,3,5,7,9,11,13,15,17,19,..., dimensions={0} | all-to-all | bytes 1572864 | tf_op jit(solution)/shard_map/cond/branch_1_fun/all_to_all | solution.py:44
  48.1 0.1 fusion
  48.2 1.9 %collective-permute-start.3 = (bf16[256,768]{1,0:T(8,128)(2,1)S(1)}, bf16[256,768]{1,0:T(8,128)(2,1)S(1)}, u32[]{:S(2)}, u32[]{:S(2)}) collective-permute-start(bf16[256,768]{1,0:T(8,128)(2,1)S(1)} %get-tuple-element.46), channel_id=1, source_target_pairs={{0,1},{1,0},{2,3},{3,2},{4,5},{5,4},{6,7},{7,6},{8,9},{9,8},{10,11... | collective-permute-start | bytes 1179656 | tf_op jit(solution)/shard_map/ppermute | solution.py:253
  50.1 1.7 %collective-permute-done.3.got = bf16[256,768]{1,0:T(8,128)(2,1)S(1)} collective-permute-done((bf16[256,768]{1,0:T(8,128)(2,1)S(1)}, bf16[256,768]{1,0:T(8,128)(2,1)S(1)}, u32[]{:S(2)}, u32[]{:S(2)}) %collective-permute-start.3) | collective-permute-done | bytes 393248 | tf_op jit(solution)/shard_map/ppermute | solution.py:253
  51.8 0.4 join_kernel.1
  52.2 13.0 %all_to_all.20 = f32[32,4,128]{2,1,0:T(4,128)S(1)} all-to-all(f32[32,4,128]{2,1,0:T(4,128)S(1)} %join_kernel.1), channel_id=1, replica_groups=mesh['ex'=16,'par'=32] {'par'}, dimensions={0} | all-to-all | bytes 131072 | tf_op jit(solution)/shard_map/all_to_all | solution.py:255
  65.3 0.6 copy.16
  (4 shorter events, 0.1 us)
Async XLA Ops:
  1.3 11.0 %collective-permute-start.2 = (bf16[3904,128]{1,0:T(8,128)(2,1)S(1)}, bf16[3904,128]{1,0:T(8,128)(2,1)S(1)}, u32[]{:S(2)}, u32[]{:S(2)}) collective-permute-start(bf16[3904,128]{1,0:T(8,128)(2,1)S(1)} %pack_kernel.1.own), channel_id=1, source_target_pairs={{0,1},{1,0},{2,3},{3,2},{4,5},{5,4},{6,7},{7,6},{8,9},{9,8},{10,11... | collective-permute-start | bytes 2998280 | tf_op jit(solution)/shard_map/ppermute | solution.py:247
  10.1 3.6 %copy-start = (bf16[4,128,128]{2,1,0:T(8,128)(2,1)S(1)}, bf16[4,128,128]{2,1,0:T(8,128)(2,1)}, u32[]{:S(2)}) copy-start(bf16[4,128,128]{2,1,0:T(8,128)(2,1)} %param.14) | copy-start | bytes 393220
  10.1 3.6 %copy-start.1 = (bf16[4,128,128]{2,1,0:T(8,128)(2,1)S(1)}, bf16[4,128,128]{2,1,0:T(8,128)(2,1)}, u32[]{:S(2)}) copy-start(bf16[4,128,128]{2,1,0:T(8,128)(2,1)} %param.15) | copy-start | bytes 393220
  10.1 3.6 %copy-start.2 = (bf16[4,128,128]{2,1,0:T(8,128)(2,1)S(1)}, bf16[4,128,128]{2,1,0:T(8,128)(2,1)}, u32[]{:S(2)}) copy-start(bf16[4,128,128]{2,1,0:T(8,128)(2,1)} %param.16) | copy-start | bytes 393220
  10.1 3.6 %copy-start.3 = (bf16[4,128,128]{2,1,0:T(8,128)(2,1)S(1)}, bf16[4,128,128]{2,1,0:T(8,128)(2,1)}, u32[]{:S(2)}) copy-start(bf16[4,128,128]{2,1,0:T(8,128)(2,1)} %param.17) | copy-start | bytes 393220
  10.2 3.6 %copy-start.4 = (bf16[4,128,128]{2,1,0:T(8,128)(2,1)S(1)}, bf16[4,128,128]{2,1,0:T(8,128)(2,1)}, u32[]{:S(2)}) copy-start(bf16[4,128,128]{2,1,0:T(8,128)(2,1)} %param.18) | copy-start | bytes 393220
  10.2 3.6 %copy-start.7 = (bf16[4,128,64]{1,2,0:T(8,128)(2,1)S(1)}, bf16[4,128,64]{1,2,0:T(8,128)(2,1)}, u32[]{:S(2)}) copy-start(bf16[4,128,64]{1,2,0:T(8,128)(2,1)} %param.24) | copy-start | bytes 196612
  48.2 3.6 %collective-permute-start.3 = (bf16[256,768]{1,0:T(8,128)(2,1)S(1)}, bf16[256,768]{1,0:T(8,128)(2,1)S(1)}, u32[]{:S(2)}, u32[]{:S(2)}) collective-permute-start(bf16[256,768]{1,0:T(8,128)(2,1)S(1)} %get-tuple-element.46), channel_id=1, source_target_pairs={{0,1},{1,0},{2,3},{3,2},{4,5},{5,4},{6,7},{7,6},{8,9},{9,8},{10,11... | collective-permute-start | bytes 1179656 | tf_op jit(solution)/shard_map/ppermute | solution.py:253

commit v7 on v6

--- a/solution.py
+++ b/solution.py
@@ -239,6 +239,17 @@
     return parts(gathered, up_right, down_left, inputs, other)
 
 
+def place_kernel(pieces, out):
+    total = [pieces[core] for core in range(2)]
+    for chip in range(1, 16):
+        total = [total[core] + pieces[2 * chip + core] for core in range(2)]
+    for e in range(4):
+        rows = total[CHAIN if e < 2 else 1 - CHAIN] * (1.0 / 128)
+        for i in range(2):
+            at = 2 * (e % 2) + i
+            out[e : e + 1, 128 * i : 128 * i + 128] = rows[at : at + 1]
+
+
 def per_device(*args):
     inputs, (lora_a, lora_b, up_left, up_right, down_left, down_right) = args[:6], args[6:]
 
@@ -253,9 +264,7 @@
     got = lax.ppermute(send, "par", PAIR)
     out = call(join_kernel, [((32, 4, 128), F32)], keep, got)[0]
     out = lax.all_to_all(out, "par", 0, 0, tiled=True)
-    out = jnp.sum(out.reshape(16, 4, 2, 128), axis=0) * (1.0 / 128)
-    out = jnp.concatenate([out[2:], out[:2]])
-    return out.reshape(4, 256)
+    return call(place_kernel, [((4, 256), F32)], out, place=jax.ShapeDtypeStruct)[0]
 
 
 def solution(mesh):

time: 66.2 us -> 66.2 us (level)
    pallas_call x3 -> x4, Pallas kernels: 3.12 us -> 3.71 us  [call(): pl.pallas_call(kernel, out_shape=tuple((place(shape, dtype) for shape, dt...]
where the time goes in v7:
time: 66.2 us; the launch traced here: 65.9 us
  blocking collectives  47.2 us (71%)
  starting transfers between devices  10.7 us (16%)
  waiting for transfers between devices  3.8 us (6%)
  Pallas kernels  3.71 us (6%)
    all_to_all x1, blocking collectives, move_rows(): lax.all_to_all(part, 'par', 0, 0, tiled=True, axis_index_groups=CHIPS)  17.5 us
    all_to_all x1, blocking collectives, spread(): lax.all_to_all(copies, axis, 0, 0, tiled=True, axis_index_groups=groups)  16.6 us
    all_to_all x1, blocking collectives, per_device(): out = lax.all_to_all(out, 'par', 0, 0, tiled=True)  13 us
    ppermute x1, starting transfers between devices, per_device(): other = lax.ppermute(own, 'par', PAIR)  8.79 us
    pallas_call x4, Pallas kernels, call(): pl.pallas_call(kernel, out_shape=tuple((place(shape, dtype) for shape, dt...  3.71 us
    ppermute x1, waiting for transfers between devices, per_device(): other = lax.ppermute(own, 'par', PAIR)  2.11 us
    ppermute x1, starting transfers between devices, per_device(): got = lax.ppermute(send, 'par', PAIR)  1.92 us
    ppermute x1, waiting for transfers between devices, per_device(): got = lax.ppermute(send, 'par', PAIR)  1.69 us
  transfers between devices with their start and end apart: 2, of which 2 were waited for; matrix products, arithmetic and copies ran while one was open for 0% of the time, Pallas kernels for 0%

profile of v7, /device:TPU:1, one launch (start us, length us, event | category | flops | bytes accessed | tf_op | source)
XLA Modules:
  0.0 65.9 jit_solution(11086434581174067278)
XLA Ops:
  0.0 1.3 %pack_kernel.1.own = bf16[3904,128]{1,0:T(8,128)(2,1)S(1)} custom-call(bf16[512,128]{1,0:T(8,128)(2,1)} %bitcast.23, bf16[512,128]{1,0:T(8,128)(2,1)} %bitcast.25, bf16[512,128]{1,0:T(8,128)(2,1)} %bitcast.27, bf16[512,128]{1,0:T(8,128)(2,1)} %bitcast.29, bf16[512,128]{1,0:T(8,128)(2,1)} %bitcast.31, bf16[512,128]{1,0:T(8,128)(2,1)} %bitcast.33, ...), custom_call_target="tpu_custom_call" | custom-call | tf_op jit(solution)/shard_map/pack_kernel/pallas_call | solution.py:27
  1.3 8.8 %collective-permute-start.2 = (bf16[3904,128]{1,0:T(8,128)(2,1)S(1)}, bf16[3904,128]{1,0:T(8,128)(2,1)S(1)}, u32[]{:S(2)}, u32[]{:S(2)}) collective-permute-start(bf16[3904,128]{1,0:T(8,128)(2,1)S(1)} %pack_kernel.1.own), channel_id=1, source_target_pairs={{0,1},{1,0},{2,3},{3,2},{4,5},{5,4},{6,7},{7,6},{8,9},{9,8},{10,11... | collective-permute-start | bytes 2998280 | tf_op jit(solution)/shard_map/ppermute | solution.py:258
  10.1 0.0 copy-start
  10.1 0.0 copy-start.1
  10.1 0.0 copy-start.2
  10.1 0.0 copy-start.3
  10.2 0.0 copy-start.4
  10.2 0.0 copy-start.7
  10.2 2.1 %collective-permute-done.2.other = bf16[3904,128]{1,0:T(8,128)(2,1)S(1)} collective-permute-done((bf16[3904,128]{1,0:T(8,128)(2,1)S(1)}, bf16[3904,128]{1,0:T(8,128)(2,1)S(1)}, u32[]{:S(2)}, u32[]{:S(2)}) %collective-permute-start.2) | collective-permute-done | bytes 999456 | tf_op jit(solution)/shard_map/ppermute | solution.py:258
  12.3 1.4 %first_kernel.1 = (bf16[16,32,768]{2,1,0:T(8,128)(2,1)}, bf16[128,128]{1,0:T(8,128)(2,1)S(1)}, bf16[3072,128]{1,0:T(8,128)(2,1)S(1)}) custom-call(bf16[3904,128]{1,0:T(8,128)(2,1)S(1)} %pack_kernel.1.own, bf16[3904,128]{1,0:T(8,128)(2,1)S(1)} %collective-permute-done.2.other), custom_call_target="tpu_custom_call" | custom-call | tf_op jit(solution)/shard_map/first_kernel/pallas_call | solution.py:27
  13.7 0.0 copy-done
  13.7 0.0 copy-done.1
  13.7 0.0 copy-done.2
  13.7 0.0 copy-done.3
  13.7 0.0 copy-done.4
  13.7 0.0 copy-done.7
  13.7 34.4 %conditional.1 = ((bf16[256,768]{1,0:T(8,128)(2,1)S(1)}, bf16[256,768]{1,0:T(8,128)(2,1)S(1)})) conditional(s32[]{:T(128)} %convert_element_type.2, (bf16[128,128]{1,0:T(8,128)(2,1)S(1)}, bf16[4,64,128]{2,1,0:T(8,128)(2,1)S(1)}, bf16[4,128,128]{2,1,0:T(8,128)(2,1)}, bf16[512,128]{1,0:T(8,128)(2,1)S(1)}, bf16[512,128]{1,0:T(8,128)(2,1)S(1)}, ...), branch_computations={%region_0.1_spmd, %region_1.3_spmd} | conditional | flops 368640 | bytes 6389786 | solution.py:263
  13.8 17.5 %all_to_all.18 = bf16[16,32,768]{2,1,0:T(8,128)(2,1)S(1)} all-to-all(bf16[16,32,768]{2,1,0:T(8,128)(2,1)} %param.1), channel_id=1, replica_groups={{0,2,4,6,8,10,12,14,16,18,20,22,24,26,28,30},{1,3,5,7,9,11,13,15,17,19,..., dimensions={0} | all-to-all | bytes 1572864 | tf_op jit(solution)/shard_map/cond/branch_1_fun/all_to_all | solution.py:224
  31.3 0.1 reduce_sum.11
  31.4 0.1 broadcast_in_dim.8
  31.5 16.6 %all_to_all.19 = bf16[16,32,768]{2,1,0:T(8,128)(2,1)S(1)} all-to-all(bf16[16,32,768]{2,1,0:T(8,128)(2,1)S(1)} %broadcast_in_dim.8), channel_id=1, replica_groups={{0,2,4,6,8,10,12,14,16,18,20,22,24,26,28,30},{1,3,5,7,9,11,13,15,17,19,..., dimensions={0} | all-to-all | bytes 1572864 | tf_op jit(solution)/shard_map/cond/branch_1_fun/all_to_all | solution.py:44
  48.1 0.1 fusion
  48.2 1.9 %collective-permute-start.3 = (bf16[256,768]{1,0:T(8,128)(2,1)S(1)}, bf16[256,768]{1,0:T(8,128)(2,1)S(1)}, u32[]{:S(2)}, u32[]{:S(2)}) collective-permute-start(bf16[256,768]{1,0:T(8,128)(2,1)S(1)} %get-tuple-element.46), channel_id=1, source_target_pairs={{0,1},{1,0},{2,3},{3,2},{4,5},{5,4},{6,7},{7,6},{8,9},{9,8},{10,11... | collective-permute-start | bytes 1179656 | tf_op jit(solution)/shard_map/ppermute | solution.py:264
  50.1 1.7 %collective-permute-done.3.got = bf16[256,768]{1,0:T(8,128)(2,1)S(1)} collective-permute-done((bf16[256,768]{1,0:T(8,128)(2,1)S(1)}, bf16[256,768]{1,0:T(8,128)(2,1)S(1)}, u32[]{:S(2)}, u32[]{:S(2)}) %collective-permute-start.3) | collective-permute-done | bytes 393248 | tf_op jit(solution)/shard_map/ppermute | solution.py:264
  51.8 0.4 join_kernel.1
  52.2 13.0 %all_to_all.20.pieces = f32[32,4,128]{2,1,0:T(4,128)S(1)} all-to-all(f32[32,4,128]{2,1,0:T(4,128)S(1)} %join_kernel.1), channel_id=1, replica_groups=mesh['ex'=16,'par'=32] {'par'}, dimensions={0} | all-to-all | bytes 131072 | tf_op jit(solution)/shard_map/all_to_all | solution.py:266
  65.3 0.6 place_kernel.1
Async XLA Ops:
  1.3 11.0 %collective-permute-start.2 = (bf16[3904,128]{1,0:T(8,128)(2,1)S(1)}, bf16[3904,128]{1,0:T(8,128)(2,1)S(1)}, u32[]{:S(2)}, u32[]{:S(2)}) collective-permute-start(bf16[3904,128]{1,0:T(8,128)(2,1)S(1)} %pack_kernel.1.own), channel_id=1, source_target_pairs={{0,1},{1,0},{2,3},{3,2},{4,5},{5,4},{6,7},{7,6},{8,9},{9,8},{10,11... | collective-permute-start | bytes 2998280 | tf_op jit(solution)/shard_map/ppermute | solution.py:258
  10.1 3.6 %copy-start = (bf16[4,128,128]{2,1,0:T(8,128)(2,1)S(1)}, bf16[4,128,128]{2,1,0:T(8,128)(2,1)}, u32[]{:S(2)}) copy-start(bf16[4,128,128]{2,1,0:T(8,128)(2,1)} %param.14) | copy-start | bytes 393220
  10.1 3.6 %copy-start.1 = (bf16[4,128,128]{2,1,0:T(8,128)(2,1)S(1)}, bf16[4,128,128]{2,1,0:T(8,128)(2,1)}, u32[]{:S(2)}) copy-start(bf16[4,128,128]{2,1,0:T(8,128)(2,1)} %param.15) | copy-start | bytes 393220
  10.1 3.6 %copy-start.2 = (bf16[4,128,128]{2,1,0:T(8,128)(2,1)S(1)}, bf16[4,128,128]{2,1,0:T(8,128)(2,1)}, u32[]{:S(2)}) copy-start(bf16[4,128,128]{2,1,0:T(8,128)(2,1)} %param.16) | copy-start | bytes 393220
  10.1 3.6 %copy-start.3 = (bf16[4,128,128]{2,1,0:T(8,128)(2,1)S(1)}, bf16[4,128,128]{2,1,0:T(8,128)(2,1)}, u32[]{:S(2)}) copy-start(bf16[4,128,128]{2,1,0:T(8,128)(2,1)} %param.17) | copy-start | bytes 393220
  10.2 3.6 %copy-start.4 = (bf16[4,128,128]{2,1,0:T(8,128)(2,1)S(1)}, bf16[4,128,128]{2,1,0:T(8,128)(2,1)}, u32[]{:S(2)}) copy-start(bf16[4,128,128]{2,1,0:T(8,128)(2,1)} %param.18) | copy-start | bytes 393220
  10.2 3.6 %copy-start.7 = (bf16[4,128,64]{1,2,0:T(8,128)(2,1)S(1)}, bf16[4,128,64]{1,2,0:T(8,128)(2,1)}, u32[]{:S(2)}) copy-start(bf16[4,128,64]{1,2,0:T(8,128)(2,1)} %param.24) | copy-start | bytes 196612
  48.2 3.6 %collective-permute-start.3 = (bf16[256,768]{1,0:T(8,128)(2,1)S(1)}, bf16[256,768]{1,0:T(8,128)(2,1)S(1)}, u32[]{:S(2)}, u32[]{:S(2)}) collective-permute-start(bf16[256,768]{1,0:T(8,128)(2,1)S(1)} %get-tuple-element.46), channel_id=1, source_target_pairs={{0,1},{1,0},{2,3},{3,2},{4,5},{5,4},{6,7},{7,6},{8,9},{9,8},{10,11... | collective-permute-start | bytes 1179656 | tf_op jit(solution)/shard_map/ppermute | solution.py:264

commit v8 on v7

--- a/solution.py
+++ b/solution.py
@@ -82,11 +82,6 @@
     return jnp.concatenate([own[at], other[at]], axis=1)
 
 
-def pick(rows, half, weight, over):
-    low, high = [dot(rows(2 + 2 * half + i), weight, 1, over) for i in range(2)]
-    return jnp.where(lax.broadcasted_iota(jnp.int32, low.shape, 1) < 64, low, high)
-
-
 def first_kernel(own, other, part, ranks, far, rows, sem):
     role = lax.rem(lax.axis_index("par") + CHAIN, 2)
     ranks[:64] = own[RANKS:ALL]
@@ -108,7 +103,12 @@
         left = jnp.concatenate([own[UL:DR], other[UL:DR]], axis=1)
         for half in range(2):
             weight = left[128 * half : 128 * half + 128]
-            put(512 + 128 * half, pick(lambda k: rows_of(own, other, k), half, weight, 1))
+            low = lax.broadcasted_iota(jnp.int32, weight.shape, 0) < 64
+            zero = jnp.zeros_like(weight)
+            weight = [jnp.where(low, weight, zero), jnp.where(low, zero, weight)]
+            grads = [rows_of(own, other, 2 + 2 * half + i) for i in range(2)]
+            weight, grads = (jnp.concatenate(v, axis=1) for v in (weight, grads))
+            put(512 + 128 * half, dot(grads, weight, 1, 1))
         hidden = rows_of(own, other, 0)
         put(0, dot(hidden, jnp.concatenate([right(0), right(1)], axis=1), 1, 0))
         put(256, dot(hidden, right(2), 1, 0))
@@ -179,8 +179,9 @@
     put(256, dot(hidden, weight(x_at, 2), 1, 0))
     put(384, dot(rows(1), weight(x_at, 3), 1, 0))
     for half in range(2):
-        pair = weight(g_at, 2 * half) + weight(g_at, 2 * half + 1)
-        put(512 + 128 * half, pick(rows, half, pair, 0))
+        pair = jnp.concatenate([weight(g_at, 2 * half + i) for i in range(2)], axis=0)
+        grads = jnp.concatenate([rows(2 + 2 * half + i) for i in range(2)], axis=1)
+        put(512 + 128 * half, dot(grads, pair, 1, 0))
 
 
 def parts(gathered, up_right, down_left, inputs, other):

time: 66.2 us -> 66.2 us (level)
  no operation moved by 1% of the time
where the time goes in v8:
time: 66.2 us; the launch traced here: 65.9 us
  blocking collectives  47.2 us (71%)
  starting transfers between devices  10.7 us (16%)
  waiting for transfers between devices  3.8 us (6%)
  Pallas kernels  3.71 us (6%)
    all_to_all x1, blocking collectives, move_rows(): lax.all_to_all(part, 'par', 0, 0, tiled=True, axis_index_groups=CHIPS)  17.5 us
    all_to_all x1, blocking collectives, spread(): lax.all_to_all(copies, axis, 0, 0, tiled=True, axis_index_groups=groups)  16.6 us
    all_to_all x1, blocking collectives, per_device(): out = lax.all_to_all(out, 'par', 0, 0, tiled=True)  13 us
    ppermute x1, starting transfers between devices, per_device(): other = lax.ppermute(own, 'par', PAIR)  8.79 us
    pallas_call x4, Pallas kernels, call(): pl.pallas_call(kernel, out_shape=tuple((place(shape, dtype) for shape, dt...  3.71 us
    ppermute x1, waiting for transfers between devices, per_device(): other = lax.ppermute(own, 'par', PAIR)  2.11 us
    ppermute x1, starting transfers between devices, per_device(): got = lax.ppermute(send, 'par', PAIR)  1.92 us
    ppermute x1, waiting for transfers between devices, per_device(): got = lax.ppermute(send, 'par', PAIR)  1.69 us
  transfers between devices with their start and end apart: 2, of which 2 were waited for; matrix products, arithmetic and copies ran while one was open for 0% of the time, Pallas kernels for 0%

profile of v8, /device:TPU:1, one launch (start us, length us, event | category | flops | bytes accessed | tf_op | source)
XLA Modules:
  0.0 65.9 jit_solution(12870409673169993108)
XLA Ops:
  0.0 1.3 %pack_kernel.1.own = bf16[3904,128]{1,0:T(8,128)(2,1)S(1)} custom-call(bf16[512,128]{1,0:T(8,128)(2,1)} %bitcast.23, bf16[512,128]{1,0:T(8,128)(2,1)} %bitcast.25, bf16[512,128]{1,0:T(8,128)(2,1)} %bitcast.27, bf16[512,128]{1,0:T(8,128)(2,1)} %bitcast.29, bf16[512,128]{1,0:T(8,128)(2,1)} %bitcast.31, bf16[512,128]{1,0:T(8,128)(2,1)} %bitcast.33, ...), custom_call_target="tpu_custom_call" | custom-call | tf_op jit(solution)/shard_map/pack_kernel/pallas_call | solution.py:27
  1.3 8.8 %collective-permute-start.2 = (bf16[3904,128]{1,0:T(8,128)(2,1)S(1)}, bf16[3904,128]{1,0:T(8,128)(2,1)S(1)}, u32[]{:S(2)}, u32[]{:S(2)}) collective-permute-start(bf16[3904,128]{1,0:T(8,128)(2,1)S(1)} %pack_kernel.1.own), channel_id=1, source_target_pairs={{0,1},{1,0},{2,3},{3,2},{4,5},{5,4},{6,7},{7,6},{8,9},{9,8},{10,11... | collective-permute-start | bytes 2998280 | tf_op jit(solution)/shard_map/ppermute | solution.py:259
  10.1 0.0 copy-start
  10.1 0.0 copy-start.1
  10.1 0.0 copy-start.2
  10.1 0.0 copy-start.3
  10.2 0.0 copy-start.4
  10.2 0.0 copy-start.7
  10.2 2.1 %collective-permute-done.2.other = bf16[3904,128]{1,0:T(8,128)(2,1)S(1)} collective-permute-done((bf16[3904,128]{1,0:T(8,128)(2,1)S(1)}, bf16[3904,128]{1,0:T(8,128)(2,1)S(1)}, u32[]{:S(2)}, u32[]{:S(2)}) %collective-permute-start.2) | collective-permute-done | bytes 999456 | tf_op jit(solution)/shard_map/ppermute | solution.py:259
  12.3 1.4 %first_kernel.1 = (bf16[16,32,768]{2,1,0:T(8,128)(2,1)}, bf16[128,128]{1,0:T(8,128)(2,1)S(1)}, bf16[3072,128]{1,0:T(8,128)(2,1)S(1)}) custom-call(bf16[3904,128]{1,0:T(8,128)(2,1)S(1)} %pack_kernel.1.own, bf16[3904,128]{1,0:T(8,128)(2,1)S(1)} %collective-permute-done.2.other), custom_call_target="tpu_custom_call" | custom-call | tf_op jit(solution)/shard_map/first_kernel/pallas_call | solution.py:27
  13.7 0.0 copy-done
  13.7 0.0 copy-done.1
  13.7 0.0 copy-done.2
  13.7 0.0 copy-done.3
  13.7 0.0 copy-done.4
  13.7 0.0 copy-done.7
  13.7 34.4 %conditional.1 = ((bf16[256,768]{1,0:T(8,128)(2,1)S(1)}, bf16[256,768]{1,0:T(8,128)(2,1)S(1)})) conditional(s32[]{:T(128)} %convert_element_type.2, (bf16[128,128]{1,0:T(8,128)(2,1)S(1)}, bf16[4,64,128]{2,1,0:T(8,128)(2,1)S(1)}, bf16[4,128,128]{2,1,0:T(8,128)(2,1)}, bf16[512,128]{1,0:T(8,128)(2,1)S(1)}, bf16[512,128]{1,0:T(8,128)(2,1)S(1)}, ...), branch_computations={%region_0.1_spmd, %region_1.3_spmd} | conditional | flops 368640 | bytes 6389786 | solution.py:264
  13.8 17.5 %all_to_all.18 = bf16[16,32,768]{2,1,0:T(8,128)(2,1)S(1)} all-to-all(bf16[16,32,768]{2,1,0:T(8,128)(2,1)} %param.1), channel_id=1, replica_groups={{0,2,4,6,8,10,12,14,16,18,20,22,24,26,28,30},{1,3,5,7,9,11,13,15,17,19,..., dimensions={0} | all-to-all | bytes 1572864 | tf_op jit(solution)/shard_map/cond/branch_1_fun/all_to_all | solution.py:225
  31.3 0.1 reduce_sum.11
  31.4 0.1 broadcast_in_dim.8
  31.5 16.6 %all_to_all.19 = bf16[16,32,768]{2,1,0:T(8,128)(2,1)S(1)} all-to-all(bf16[16,32,768]{2,1,0:T(8,128)(2,1)S(1)} %broadcast_in_dim.8), channel_id=1, replica_groups={{0,2,4,6,8,10,12,14,16,18,20,22,24,26,28,30},{1,3,5,7,9,11,13,15,17,19,..., dimensions={0} | all-to-all | bytes 1572864 | tf_op jit(solution)/shard_map/cond/branch_1_fun/all_to_all | solution.py:44
  48.1 0.1 fusion
  48.2 1.9 %collective-permute-start.3 = (bf16[256,768]{1,0:T(8,128)(2,1)S(1)}, bf16[256,768]{1,0:T(8,128)(2,1)S(1)}, u32[]{:S(2)}, u32[]{:S(2)}) collective-permute-start(bf16[256,768]{1,0:T(8,128)(2,1)S(1)} %get-tuple-element.46), channel_id=1, source_target_pairs={{0,1},{1,0},{2,3},{3,2},{4,5},{5,4},{6,7},{7,6},{8,9},{9,8},{10,11... | collective-permute-start | bytes 1179656 | tf_op jit(solution)/shard_map/ppermute | solution.py:265
  50.1 1.7 %collective-permute-done.3.got = bf16[256,768]{1,0:T(8,128)(2,1)S(1)} collective-permute-done((bf16[256,768]{1,0:T(8,128)(2,1)S(1)}, bf16[256,768]{1,0:T(8,128)(2,1)S(1)}, u32[]{:S(2)}, u32[]{:S(2)}) %collective-permute-start.3) | collective-permute-done | bytes 393248 | tf_op jit(solution)/shard_map/ppermute | solution.py:265
  51.8 0.4 join_kernel.1
  52.2 13.0 %all_to_all.20.pieces = f32[32,4,128]{2,1,0:T(4,128)S(1)} all-to-all(f32[32,4,128]{2,1,0:T(4,128)S(1)} %join_kernel.1), channel_id=1, replica_groups=mesh['ex'=16,'par'=32] {'par'}, dimensions={0} | all-to-all | bytes 131072 | tf_op jit(solution)/shard_map/all_to_all | solution.py:267
  65.2 0.6 place_kernel.1
Async XLA Ops:
  1.3 11.0 %collective-permute-start.2 = (bf16[3904,128]{1,0:T(8,128)(2,1)S(1)}, bf16[3904,128]{1,0:T(8,128)(2,1)S(1)}, u32[]{:S(2)}, u32[]{:S(2)}) collective-permute-start(bf16[3904,128]{1,0:T(8,128)(2,1)S(1)} %pack_kernel.1.own), channel_id=1, source_target_pairs={{0,1},{1,0},{2,3},{3,2},{4,5},{5,4},{6,7},{7,6},{8,9},{9,8},{10,11... | collective-permute-start | bytes 2998280 | tf_op jit(solution)/shard_map/ppermute | solution.py:259
  10.1 3.6 %copy-start = (bf16[4,128,128]{2,1,0:T(8,128)(2,1)S(1)}, bf16[4,128,128]{2,1,0:T(8,128)(2,1)}, u32[]{:S(2)}) copy-start(bf16[4,128,128]{2,1,0:T(8,128)(2,1)} %param.14) | copy-start | bytes 393220
  10.1 3.6 %copy-start.1 = (bf16[4,128,128]{2,1,0:T(8,128)(2,1)S(1)}, bf16[4,128,128]{2,1,0:T(8,128)(2,1)}, u32[]{:S(2)}) copy-start(bf16[4,128,128]{2,1,0:T(8,128)(2,1)} %param.15) | copy-start | bytes 393220
  10.1 3.6 %copy-start.2 = (bf16[4,128,128]{2,1,0:T(8,128)(2,1)S(1)}, bf16[4,128,128]{2,1,0:T(8,128)(2,1)}, u32[]{:S(2)}) copy-start(bf16[4,128,128]{2,1,0:T(8,128)(2,1)} %param.16) | copy-start | bytes 393220
  10.1 3.6 %copy-start.3 = (bf16[4,128,128]{2,1,0:T(8,128)(2,1)S(1)}, bf16[4,128,128]{2,1,0:T(8,128)(2,1)}, u32[]{:S(2)}) copy-start(bf16[4,128,128]{2,1,0:T(8,128)(2,1)} %param.17) | copy-start | bytes 393220
  10.2 3.6 %copy-start.4 = (bf16[4,128,128]{2,1,0:T(8,128)(2,1)S(1)}, bf16[4,128,128]{2,1,0:T(8,128)(2,1)}, u32[]{:S(2)}) copy-start(bf16[4,128,128]{2,1,0:T(8,128)(2,1)} %param.18) | copy-start | bytes 393220
  10.2 3.6 %copy-start.7 = (bf16[4,128,64]{1,2,0:T(8,128)(2,1)S(1)}, bf16[4,128,64]{1,2,0:T(8,128)(2,1)}, u32[]{:S(2)}) copy-start(bf16[4,128,64]{1,2,0:T(8,128)(2,1)} %param.24) | copy-start | bytes 196612
  48.2 3.6 %collective-permute-start.3 = (bf16[256,768]{1,0:T(8,128)(2,1)S(1)}, bf16[256,768]{1,0:T(8,128)(2,1)S(1)}, u32[]{:S(2)}, u32[]{:S(2)}) collective-permute-start(bf16[256,768]{1,0:T(8,128)(2,1)S(1)} %get-tuple-element.46), channel_id=1, source_target_pairs={{0,1},{1,0},{2,3},{3,2},{4,5},{5,4},{6,7},{7,6},{8,9},{9,8},{10,11... | collective-permute-start | bytes 1179656 | tf_op jit(solution)/shard_map/ppermute | solution.py:265

commit v9 on v8

--- a/solution.py
+++ b/solution.py
@@ -84,8 +84,6 @@
 
 def first_kernel(own, other, part, ranks, far, rows, sem):
     role = lax.rem(lax.axis_index("par") + CHAIN, 2)
-    ranks[:64] = own[RANKS:ALL]
-    ranks[64:] = other[RANKS:ALL]
     copies = []
 
     def put(at, value):
@@ -118,9 +116,16 @@
 
     @pl.when(role == 1)
     def _():
-        copy = pltpu.make_async_copy(other.at[pl.ds(0, UL)], far, sem)
-        copy.start()
-        copy.wait()
+        ends = [
+            (own.at[pl.ds(RANKS, 64)], ranks.at[pl.ds(0, 64)]),
+            (other.at[pl.ds(RANKS, 64)], ranks.at[pl.ds(64, 64)]),
+            (other.at[pl.ds(0, UL)], far),
+        ]
+        moves = [pltpu.make_async_copy(a, b, sem) for a, b in ends]
+        for move in moves:
+            move.start()
+        for move in moves:
+            move.wait()
 
 
 def first(own, other):
@@ -132,7 +137,7 @@
         other,
         scratch=[pltpu.VMEM((16, 32, 768), BF), pltpu.SemaphoreType.DMA],
         place=jax.ShapeDtypeStruct,
-        out_specs=(HBM, VMEM, HBM),
+        out_specs=(HBM, HBM, HBM),
     )
 
 

time: 66.2 us -> 66.2 us (level)
  no operation moved by 1% of the time
where the time goes in v9:
time: 66.2 us; the launch traced here: 65.9 us
  blocking collectives  47.2 us (71%)
  starting transfers between devices  10.7 us (16%)
  waiting for transfers between devices  3.8 us (6%)
  Pallas kernels  3.71 us (6%)
    all_to_all x1, blocking collectives, move_rows(): lax.all_to_all(part, 'par', 0, 0, tiled=True, axis_index_groups=CHIPS)  17.5 us
    all_to_all x1, blocking collectives, spread(): lax.all_to_all(copies, axis, 0, 0, tiled=True, axis_index_groups=groups)  16.6 us
    all_to_all x1, blocking collectives, per_device(): out = lax.all_to_all(out, 'par', 0, 0, tiled=True)  13 us
    ppermute x1, starting transfers between devices, per_device(): other = lax.ppermute(own, 'par', PAIR)  8.79 us
    pallas_call x4, Pallas kernels, call(): pl.pallas_call(kernel, out_shape=tuple((place(shape, dtype) for shape, dt...  3.71 us
    ppermute x1, waiting for transfers between devices, per_device(): other = lax.ppermute(own, 'par', PAIR)  2.11 us
    ppermute x1, starting transfers between devices, per_device(): got = lax.ppermute(send, 'par', PAIR)  1.92 us
    ppermute x1, waiting for transfers between devices, per_device(): got = lax.ppermute(send, 'par', PAIR)  1.69 us
  transfers between devices with their start and end apart: 2, of which 2 were waited for; matrix products, arithmetic and copies ran while one was open for 0% of the time, Pallas kernels for 0%

profile of v9, /device:TPU:1, one launch (start us, length us, event | category | flops | bytes accessed | tf_op | source)
XLA Modules:
  0.0 65.9 jit_solution(6253877108448154052)
XLA Ops:
  0.0 1.3 %pack_kernel.1.own = bf16[3904,128]{1,0:T(8,128)(2,1)S(1)} custom-call(bf16[512,128]{1,0:T(8,128)(2,1)} %bitcast.23, bf16[512,128]{1,0:T(8,128)(2,1)} %bitcast.25, bf16[512,128]{1,0:T(8,128)(2,1)} %bitcast.27, bf16[512,128]{1,0:T(8,128)(2,1)} %bitcast.29, bf16[512,128]{1,0:T(8,128)(2,1)} %bitcast.31, bf16[512,128]{1,0:T(8,128)(2,1)} %bitcast.33, ...), custom_call_target="tpu_custom_call" | custom-call | tf_op jit(solution)/shard_map/pack_kernel/pallas_call | solution.py:27
  1.3 8.8 %collective-permute-start.2 = (bf16[3904,128]{1,0:T(8,128)(2,1)S(1)}, bf16[3904,128]{1,0:T(8,128)(2,1)S(1)}, u32[]{:S(2)}, u32[]{:S(2)}) collective-permute-start(bf16[3904,128]{1,0:T(8,128)(2,1)S(1)} %pack_kernel.1.own), channel_id=1, source_target_pairs={{0,1},{1,0},{2,3},{3,2},{4,5},{5,4},{6,7},{7,6},{8,9},{9,8},{10,11... | collective-permute-start | bytes 2998280 | tf_op jit(solution)/shard_map/ppermute | solution.py:264
  10.1 0.0 copy-start
  10.1 0.0 copy-start.1
  10.1 0.0 copy-start.2
  10.1 0.0 copy-start.3
  10.2 0.0 copy-start.4
  10.2 0.0 copy-start.7
  10.2 2.1 %collective-permute-done.2.other = bf16[3904,128]{1,0:T(8,128)(2,1)S(1)} collective-permute-done((bf16[3904,128]{1,0:T(8,128)(2,1)S(1)}, bf16[3904,128]{1,0:T(8,128)(2,1)S(1)}, u32[]{:S(2)}, u32[]{:S(2)}) %collective-permute-start.2) | collective-permute-done | bytes 999456 | tf_op jit(solution)/shard_map/ppermute | solution.py:264
  12.3 1.4 %first_kernel.1 = (bf16[16,32,768]{2,1,0:T(8,128)(2,1)}, bf16[128,128]{1,0:T(8,128)(2,1)S(1)}, bf16[3072,128]{1,0:T(8,128)(2,1)S(1)}) custom-call(bf16[3904,128]{1,0:T(8,128)(2,1)S(1)} %pack_kernel.1.own, bf16[3904,128]{1,0:T(8,128)(2,1)S(1)} %collective-permute-done.2.other), custom_call_target="tpu_custom_call" | custom-call | tf_op jit(solution)/shard_map/first_kernel/pallas_call | solution.py:27
  13.7 0.0 copy-done
  13.7 0.0 copy-done.1
  13.7 0.0 copy-done.2
  13.7 0.0 copy-done.3
  13.7 0.0 copy-done.4
  13.7 0.0 copy-done.7
  13.7 34.4 %conditional.1 = ((bf16[256,768]{1,0:T(8,128)(2,1)S(1)}, bf16[256,768]{1,0:T(8,128)(2,1)S(1)})) conditional(s32[]{:T(128)} %convert_element_type.2, (bf16[128,128]{1,0:T(8,128)(2,1)S(1)}, bf16[4,64,128]{2,1,0:T(8,128)(2,1)S(1)}, bf16[4,128,128]{2,1,0:T(8,128)(2,1)}, bf16[512,128]{1,0:T(8,128)(2,1)S(1)}, bf16[512,128]{1,0:T(8,128)(2,1)S(1)}, ...), branch_computations={%region_0.1_spmd, %region_1.3_spmd} | conditional | flops 368640 | bytes 6389786 | solution.py:269
  13.8 17.5 %all_to_all.18 = bf16[16,32,768]{2,1,0:T(8,128)(2,1)S(1)} all-to-all(bf16[16,32,768]{2,1,0:T(8,128)(2,1)} %param.1), channel_id=1, replica_groups={{0,2,4,6,8,10,12,14,16,18,20,22,24,26,28,30},{1,3,5,7,9,11,13,15,17,19,..., dimensions={0} | all-to-all | bytes 1572864 | tf_op jit(solution)/shard_map/cond/branch_1_fun/all_to_all | solution.py:230
  31.3 0.1 reduce_sum.11
  31.4 0.1 broadcast_in_dim.8
  31.5 16.6 %all_to_all.19 = bf16[16,32,768]{2,1,0:T(8,128)(2,1)S(1)} all-to-all(bf16[16,32,768]{2,1,0:T(8,128)(2,1)S(1)} %broadcast_in_dim.8), channel_id=1, replica_groups={{0,2,4,6,8,10,12,14,16,18,20,22,24,26,28,30},{1,3,5,7,9,11,13,15,17,19,..., dimensions={0} | all-to-all | bytes 1572864 | tf_op jit(solution)/shard_map/cond/branch_1_fun/all_to_all | solution.py:44
  48.1 0.1 fusion
  48.2 1.9 %collective-permute-start.3 = (bf16[256,768]{1,0:T(8,128)(2,1)S(1)}, bf16[256,768]{1,0:T(8,128)(2,1)S(1)}, u32[]{:S(2)}, u32[]{:S(2)}) collective-permute-start(bf16[256,768]{1,0:T(8,128)(2,1)S(1)} %get-tuple-element.46), channel_id=1, source_target_pairs={{0,1},{1,0},{2,3},{3,2},{4,5},{5,4},{6,7},{7,6},{8,9},{9,8},{10,11... | collective-permute-start | bytes 1179656 | tf_op jit(solution)/shard_map/ppermute | solution.py:270
  50.1 1.7 %collective-permute-done.3.got = bf16[256,768]{1,0:T(8,128)(2,1)S(1)} collective-permute-done((bf16[256,768]{1,0:T(8,128)(2,1)S(1)}, bf16[256,768]{1,0:T(8,128)(2,1)S(1)}, u32[]{:S(2)}, u32[]{:S(2)}) %collective-permute-start.3) | collective-permute-done | bytes 393248 | tf_op jit(solution)/shard_map/ppermute | solution.py:270
  51.8 0.4 join_kernel.1
  52.2 13.0 %all_to_all.20.pieces = f32[32,4,128]{2,1,0:T(4,128)S(1)} all-to-all(f32[32,4,128]{2,1,0:T(4,128)S(1)} %join_kernel.1), channel_id=1, replica_groups=mesh['ex'=16,'par'=32] {'par'}, dimensions={0} | all-to-all | bytes 131072 | tf_op jit(solution)/shard_map/all_to_all | solution.py:272
  65.3 0.6 place_kernel.1
Async XLA Ops:
  1.3 11.0 %collective-permute-start.2 = (bf16[3904,128]{1,0:T(8,128)(2,1)S(1)}, bf16[3904,128]{1,0:T(8,128)(2,1)S(1)}, u32[]{:S(2)}, u32[]{:S(2)}) collective-permute-start(bf16[3904,128]{1,0:T(8,128)(2,1)S(1)} %pack_kernel.1.own), channel_id=1, source_target_pairs={{0,1},{1,0},{2,3},{3,2},{4,5},{5,4},{6,7},{7,6},{8,9},{9,8},{10,11... | collective-permute-start | bytes 2998280 | tf_op jit(solution)/shard_map/ppermute | solution.py:264
  10.1 3.6 %copy-start = (bf16[4,128,128]{2,1,0:T(8,128)(2,1)S(1)}, bf16[4,128,128]{2,1,0:T(8,128)(2,1)}, u32[]{:S(2)}) copy-start(bf16[4,128,128]{2,1,0:T(8,128)(2,1)} %param.14) | copy-start | bytes 393220
  10.1 3.6 %copy-start.1 = (bf16[4,128,128]{2,1,0:T(8,128)(2,1)S(1)}, bf16[4,128,128]{2,1,0:T(8,128)(2,1)}, u32[]{:S(2)}) copy-start(bf16[4,128,128]{2,1,0:T(8,128)(2,1)} %param.15) | copy-start | bytes 393220
  10.1 3.6 %copy-start.2 = (bf16[4,128,128]{2,1,0:T(8,128)(2,1)S(1)}, bf16[4,128,128]{2,1,0:T(8,128)(2,1)}, u32[]{:S(2)}) copy-start(bf16[4,128,128]{2,1,0:T(8,128)(2,1)} %param.16) | copy-start | bytes 393220
  10.1 3.6 %copy-start.3 = (bf16[4,128,128]{2,1,0:T(8,128)(2,1)S(1)}, bf16[4,128,128]{2,1,0:T(8,128)(2,1)}, u32[]{:S(2)}) copy-start(bf16[4,128,128]{2,1,0:T(8,128)(2,1)} %param.17) | copy-start | bytes 393220
  10.2 3.6 %copy-start.4 = (bf16[4,128,128]{2,1,0:T(8,128)(2,1)S(1)}, bf16[4,128,128]{2,1,0:T(8,128)(2,1)}, u32[]{:S(2)}) copy-start(bf16[4,128,128]{2,1,0:T(8,128)(2,1)} %param.18) | copy-start | bytes 393220
  10.2 3.6 %copy-start.7 = (bf16[4,128,64]{1,2,0:T(8,128)(2,1)S(1)}, bf16[4,128,64]{1,2,0:T(8,128)(2,1)}, u32[]{:S(2)}) copy-start(bf16[4,128,64]{1,2,0:T(8,128)(2,1)} %param.24) | copy-start | bytes 196612
  48.2 3.6 %collective-permute-start.3 = (bf16[256,768]{1,0:T(8,128)(2,1)S(1)}, bf16[256,768]{1,0:T(8,128)(2,1)S(1)}, u32[]{:S(2)}, u32[]{:S(2)}) collective-permute-start(bf16[256,768]{1,0:T(8,128)(2,1)S(1)} %get-tuple-element.46), channel_id=1, source_target_pairs={{0,1},{1,0},{2,3},{3,2},{4,5},{5,4},{6,7},{7,6},{8,9},{9,8},{10,11... | collective-permute-start | bytes 1179656 | tf_op jit(solution)/shard_map/ppermute | solution.py:270
